TPU v7x, 128 devices: a whole 4x4x4 slice. The times are simulated.
128 devices in a mesh: row: 16 (over z, x), col: 8 (over y, core).
Axes of the slice: x: 4, y: 4, z: 4, core: 2. Of those that a mesh axis runs over, the one named last changes fastest.
Arguments:
- tokens: bfloat16 [2048, 4096], P('row', 'col'), may hold values from -6 to 6
- cotangent: bfloat16 [2048, 4096], P('row', 'col'), may hold values from -6 to 6
- norm_gain: float32 [4096], P('col'), may hold values from 0.5 to 2
- gate_weight: bfloat16 [4096, 14336], P('col', 'row'), may hold values from -0.09375 to 0.09375
- up_weight: bfloat16 [4096, 14336], P('col', 'row'), may hold values from -0.09375 to 0.09375
- down_weight: bfloat16 [14336, 4096], P('row', 'col'), may hold values from -0.046875 to 0.046875
- gate_blocks: int32 [32, 112], P('col', 'row'), may hold values 0 or 1
- up_blocks: int32 [32, 112], P('col', 'row'), may hold values 0 or 1
- down_blocks: int32 [112, 32], P('row', 'col'), may hold values 0 or 1
Outputs:
- mixed: bfloat16 [2048, 4096], P('row', 'col')
- input_gradient: bfloat16 [2048, 4096], P('row', 'col')
- gate_gradient: bfloat16 [4096, 14336], P('col', 'row')
- up_gradient: bfloat16 [4096, 14336], P('col', 'row')
- down_gradient: bfloat16 [14336, 4096], P('row', 'col')
Inputs may be any that keep to these rules, and one draw needn't show every extreme that they name: `gate_blocks`: 1 keeps a block of 128 x 128 weights, 0 prunes it. `up_blocks`: 1 keeps a block of 128 x 128 weights, 0 prunes it. `down_blocks`: 1 keeps a block of 128 x 128 weights, 0 prunes it.
All inputs are finite; a program needn't handle non-finite values.
Results may differ from a plain program's by a relative error of at most 0.013.
Values may be sent and summed in bfloat16 or wider, within the bound.
A program may use at most 128 MiB of HBM per device.

v0:
```python
import jax
import jax.numpy as jnp
from jax import lax
from jax.sharding import PartitionSpec as P

epsilon = 1e-05


def expand(weight, mask):
    mask_rows, mask_cols = mask.shape
    height = weight.shape[0] // mask_rows
    breadth = weight.shape[1] // mask_cols
    expanded = jnp.broadcast_to(mask[:, None, :, None], (mask_rows, height, mask_cols, breadth))
    return expanded.reshape(weight.shape)


def shards(
    tokens,
    cotangent,
    norm_gain,
    gate_weight,
    up_weight,
    down_weight,
    gate_blocks,
    up_blocks,
    down_blocks,
):
    gate_keep = expand(gate_weight, gate_blocks)
    up_keep = expand(up_weight, up_blocks)
    down_keep = expand(down_weight, down_blocks)
    gate_masked = gate_weight * gate_keep.astype(jnp.bfloat16)
    up_masked = up_weight * up_keep.astype(jnp.bfloat16)
    down_masked = down_weight * down_keep.astype(jnp.bfloat16)
    tok_rows, width_local = tokens.shape
    ff_local = gate_weight.shape[1]
    model_width = width_local * lax.axis_size("col")
    stacked = jnp.stack([tokens, cotangent], axis=0)
    contract = (((0,), (0,)), ((), ()))
    pieces = lax.all_gather(stacked, "row", axis=1, tiled=True)
    raw_piece = pieces[0]
    cot_piece = pieces[1]
    raw_float = raw_piece.astype(jnp.float32)
    scaled_piece = (raw_float * norm_gain).astype(jnp.bfloat16)
    products = [
        jnp.dot(scaled_piece, gate_masked, preferred_element_type=jnp.float32),
        jnp.dot(scaled_piece, up_masked, preferred_element_type=jnp.float32),
    ]
    products.append(jnp.dot(cot_piece, down_masked.T, preferred_element_type=jnp.float32))
    partial_sums = jnp.concatenate(products, axis=1)
    square_sums = jnp.sum(raw_float * raw_float, axis=1)
    partial_sums, square_sums, scaled_all, cot_all = (
        partial_sums,
        square_sums,
        scaled_piece,
        cot_piece,
    )
    partial_local, squares_local = (
        lax.psum_scatter(partial_sums, "col", scatter_dimension=0, tiled=True),
        lax.psum_scatter(square_sums, "col", scatter_dimension=0, tiled=True),
    )
    inv_rms = 1.0 / jnp.sqrt(squares_local / model_width + epsilon)
    pre_gate = partial_local[:, :ff_local]
    pre_up = partial_local[:, ff_local : 2 * ff_local]
    back_hidden = partial_local[:, 2 * ff_local :]
    factor = inv_rms[:, None]
    gate = factor * pre_gate
    up_value = factor * pre_up
    sigma = jax.nn.sigmoid(gate)
    activ = gate * sigma
    hidden = (activ * up_value).astype(jnp.bfloat16)
    d_gate = back_hidden * up_value * sigma * (1.0 + gate * (1.0 - sigma))
    d_up = back_hidden * activ
    gate_pull = (factor * d_gate).astype(jnp.bfloat16)
    up_pull = (factor * d_up).astype(jnp.bfloat16)
    rms_part = jnp.sum(d_gate * pre_gate + d_up * pre_up, axis=1)
    rms_all, inv_all = (
        lax.all_gather(rms_part, "col", axis=0, tiled=True),
        lax.all_gather(inv_rms, "col", axis=0, tiled=True),
    )
    lanes = jnp.stack([hidden, gate_pull, up_pull], axis=1)
    piece = lax.all_gather(lanes, "col", axis=0, tiled=True)
    hidden_piece = piece[:, 0]
    gate_piece = piece[:, 1]
    up_piece = piece[:, 2]
    forward = jnp.dot(hidden_piece, down_masked, preferred_element_type=jnp.float32)
    backward = jnp.dot(gate_piece, gate_masked.T, preferred_element_type=jnp.float32) + jnp.dot(
        up_piece, up_masked.T, preferred_element_type=jnp.float32
    )
    projected = jnp.concatenate([forward, backward], axis=1)
    down_total = lax.dot_general(
        hidden_piece, cot_all, contract, preferred_element_type=jnp.float32
    )
    gate_total = lax.dot_general(
        scaled_all, gate_piece, contract, preferred_element_type=jnp.float32
    )
    up_total = lax.dot_general(scaled_all, up_piece, contract, preferred_element_type=jnp.float32)
    projected, down_total, gate_total, up_total = (projected, down_total, gate_total, up_total)
    proj_rows, rms_rows = (
        lax.psum_scatter(
            projected.astype(jnp.bfloat16), "row", scatter_dimension=0, tiled=True
        ).astype(jnp.float32),
        lax.psum_scatter(
            rms_all.astype(jnp.bfloat16), "row", scatter_dimension=0, tiled=True
        ).astype(jnp.float32),
    )
    first_row = lax.axis_index("row") * tok_rows
    inv_rows = lax.dynamic_slice_in_dim(inv_all, first_row, tok_rows, 0)
    raw_float = tokens.astype(jnp.float32)
    mixed = (raw_float + proj_rows[:, :width_local]).astype(jnp.bfloat16)
    correction = raw_float * (inv_rows * inv_rows * inv_rows * rms_rows / model_width)[:, None]
    input_gradient = (
        cotangent.astype(jnp.float32) + norm_gain * proj_rows[:, width_local:] - correction
    ).astype(jnp.bfloat16)
    gate_gradient = (gate_keep.astype(jnp.float32) * gate_total).astype(jnp.bfloat16)
    up_gradient = (up_keep.astype(jnp.float32) * up_total).astype(jnp.bfloat16)
    down_gradient = (down_keep.astype(jnp.float32) * down_total).astype(jnp.bfloat16)
    return (mixed, input_gradient, gate_gradient, up_gradient, down_gradient)


def solution(mesh):
    in_specs = (
        P("row", "col"),
        P("row", "col"),
        P("col"),
        P("col", "row"),
        P("col", "row"),
        P("row", "col"),
        P("col", "row"),
        P("col", "row"),
        P("row", "col"),
    )
    out_specs = (
        P("row", "col"),
        P("row", "col"),
        P("col", "row"),
        P("col", "row"),
        P("row", "col"),
    )
    return jax.shard_map(shards, mesh=mesh, in_specs=in_specs, out_specs=out_specs, check_vma=False)
```

profile of v0, /device:TPU:1, one launch (start us, length us, event | category | flops | bytes accessed | tf_op | source)
XLA Modules:
  0.0 376.2 jit_solution(10860350215624052370)
XLA Ops:
  7.2 0.0 all-gather.5.cloned.1.call-start
  7.2 1.7 pad_maximum_fusion.3
  9.0 0.0 reduce-scatter.5.cloned.1.call-start
  9.0 0.8 fusion.42
  9.8 0.1 copy.37
  9.9 1.5 copy.38
  11.3 0.8 fusion.43
  12.1 0.1 copy.35
  12.2 1.5 copy.36
  13.7 0.1 copy.39
  13.8 51.9 %all-gather.5.cloned.1.call-done = bf16[2,2048,512]{2,1,0:T(8,128)(2,1)} async-done(((bf16[2,128,512]{2,1,0:T(8,128)(2,1)}), bf16[2,2048,512]{2,1,0:T(8,128)(2,1)}) %all-gather.5.cloned.1.call-update) | async-done | bytes 4194320 | tf_op jit(solution)/shard_map/all_gather | solution.py:39
  65.7 0.3 broadcast_in_dim.13
  66.0 3.8 %fusion.16 = f32[2048,896]{0,1:T(8,128)S(1)} fusion(f32[512]{0:T(512)S(1)} %copy-done.11, bf16[2,2048,512]{2,1,0:T(8,128)(2,1)} %all-gather.5.cloned.1.call-done, bf16[512,896]{0,1:T(8,128)(2,1)S(1)} %copy.38, bf16[112,8,4,128]{3,2,1,0:T(4,128)(2,1)S(1)} %bitcast.110), kind=kOutput, calls=%fused_computation.23 | convolution fusion | flops 1882652672 | bytes 11274240 | tf_op jit(solution)/shard_map/dot_general | solution.py:46
  69.9 0.3 broadcast_in_dim.12
  70.2 2.1 fusion.18
  72.3 0.3 broadcast_in_dim.14
  72.7 2.1 fusion.13
  74.8 9.6 %pad_maximum_fusion = f32[2048,2688]{0,1:T(8,128)} fusion(f32[2048,896]{0,1:T(8,128)S(1)} %fusion.13, f32[2048,896]{0,1:T(8,128)S(1)} %fusion.16, f32[2048,896]{0,1:T(8,128)S(1)} %fusion.18), kind=kLoop, calls=%fused_computation | loop fusion | flops 11010048 | bytes 44040192 | tf_op jit(solution)/shard_map/concatenate | solution.py:49
  84.4 0.0 all-gather.7.cloned.1.call-start
  84.5 0.6 copy-done.15
  85.1 0.6 dynamic-slice
  86.3 2.1 fusion.2
  88.4 12.8 %all-reduce = f32[2048]{0:T(1024)S(1)} all-reduce(f32[2048]{0:T(1024)S(1)} %fusion.2), channel_id=2, replica_groups=mesh['row'=16,'col'=8] {'col'}, use_global_device_ids=true, to_apply=%region_1.0.clone | all-reduce | flops 2048 | bytes 16384
  101.2 0.1 fusion.38
  101.3 99.0 %reduce-scatter.5.cloned.1.call-done = f32[256,2688]{0,1:T(8,128)} async-done(((f32[2048,2688]{0,1:T(8,128)}), f32[256,2688]{0,1:T(8,128)}) %reduce-scatter.5.cloned.1.call-update) | async-done | bytes 2752528 | tf_op jit(solution)/shard_map/reduce_scatter | solution.py:58
  200.3 2.4 fusion.30
  202.7 0.1 fusion.31
  202.8 1.2 pad_maximum_fusion.2
  204.0 0.0 all-gather.7.cloned.1.call-update
  204.0 0.2 reduce-scatter.7.cloned.1.call-start
  204.3 65.7 %all-gather.7.cloned.1.call-done = bf16[2048,3,896]{0,2,1:T(8,128)(2,1)} async-done(((bf16[256,3,896]{0,2,1:T(8,128)(2,1)}), bf16[2048,3,896]{0,2,1:T(8,128)(2,1)}) %all-gather.7.cloned.1.call-update) | async-done | bytes 11010064 | tf_op jit(solution)/shard_map/all_gather | solution.py:81
  270.0 4.9 %fusion.8 = f32[2048,512]{0,1:T(8,128)S(1)} fusion(bf16[2048,3,896]{0,2,1:T(8,128)(2,1)} %all-gather.7.cloned.1.call-done, bf16[512,896]{0,1:T(8,128)(2,1)S(1)} %copy.36, bf16[112,8,4,128]{3,2,1,0:T(4,128)(2,1)} %bitcast.113), kind=kOutput, calls=%fused_computation.16 | convolution fusion | flops 1879506944 | bytes 9699328 | tf_op jit(solution)/shard_map/dot_general | solution.py:86
  274.9 1.1 copy-done.13
  276.0 2.4 fusion.11
  278.4 2.5 add_convert_fusion
  281.0 2.6 pad_maximum_fusion.1
  283.5 6.4 %copy.48 = bf16[2048,1024]{1,0:T(8,128)(2,1)} copy(bf16[2048,1024]{0,1:T(8,128)(2,1)} %pad_maximum_fusion.1) | data formatting | bytes 8388608
  289.9 0.0 reduce-scatter.7.cloned.1.call-update
  290.0 0.9 copy-done.9
  290.8 0.1 copy.34
  291.0 0.1 copy.40
  291.1 0.6 dynamic-slice.2
  292.3 0.1 copy.43
  292.4 0.3 broadcast_in_dim.32
  292.7 0.1 copy.69
  292.9 1.7 copy.44
  294.6 0.1 copy.41
  294.7 0.3 broadcast_in_dim.15
  295.0 0.1 copy.70
  295.2 1.7 copy.42
  296.9 0.1 copy.45
  297.0 9.8 %all-gather = f32[8,1,256]{2,1,0:T(1,128)S(1)} all-gather(f32[1,1,256]{2,1,0:T(1,128)S(1)} %bitcast.121), channel_id=1, replica_groups=mesh['row'=16,'col'=8] {'col'}, dimensions={0}, use_global_device_ids=true | all-gather | bytes 9216 | tf_op jit(solution)/shard_map/all_gather | solution.py:78
  306.8 8.1 %all-gather.1 = bf16[8,1,256]{2,1,0:T(2,128)(2,1)S(1)} all-gather(bf16[1,1,256]{2,1,0:T(2,128)(2,1)S(1)} %convert.11), channel_id=1, replica_groups=mesh['row'=16,'col'=8] {'col'}, dimensions={0}, use_global_device_ids=true | all-gather | bytes 4608 | tf_op jit(solution)/shard_map/all_gather | solution.py:77
  314.9 33.8 %all-reduce.1 = bf16[2048]{0:T(1024)(128)(2,1)S(1)} all-reduce(bf16[2048]{0:T(1024)(128)(2,1)S(1)} %bitcast.120), channel_id=5, replica_groups=mesh['row'=16,'col'=8] {'row'}, use_global_device_ids=true, to_apply=%region_5.0.clone | all-reduce | flops 2048 | bytes 8192
  348.8 0.1 fusion.40
  348.8 0.3 broadcast_in_dim.33
  349.2 5.8 %fusion.20 = bf16[896,512]{1,0:T(8,128)(2,1)} fusion(f32[112,8,4,128]{3,2,1,0:T(4,128)S(1)} %bitcast.116, bf16[2,2048,512]{2,1,0:T(8,128)(2,1)} %all-gather.5.cloned.1.call-done, bf16[2048,3,896]{0,2,1:T(8,128)(2,1)} %all-gather.7.cloned.1.call-done), kind=kOutput, calls=%fused_computation.26 | convolution fusion | flops 1879965696 | bytes 8519680 | tf_op jit(solution)/shard_map/dot_general | solution.py:90
  355.0 5.5 %multiply_convert_fusion = bf16[512,896]{1,0:T(8,128)(2,1)} fusion(f32[512,896]{1,0:T(8,128)S(1)} %copy-done.5, bf16[2048,3,896]{0,2,1:T(8,128)(2,1)} %all-gather.7.cloned.1.call-done, f32[512]{0:T(512)S(1)} %copy-done.11, bf16[2,2048,512]{2,1,0:T(8,128)(2,1)S(1)} %copy-done.1), kind=kOutput, calls=%fused_computation.29 | convolution fusion | flops 1883111424 | bytes 8521728 | tf_op jit(solution)/shard_map/dot_general | solution.py:96
  360.6 5.4 %multiply_convert_fusion.1 = bf16[512,896]{1,0:T(8,128)(2,1)} fusion(f32[512,896]{1,0:T(8,128)S(1)} %copy-done.6, bf16[2048,3,896]{0,2,1:T(8,128)(2,1)} %all-gather.7.cloned.1.call-done, f32[512]{0:T(512)S(1)} %copy-done.11, bf16[2,2048,512]{2,1,0:T(8,128)(2,1)S(1)} %copy-done.1), kind=kOutput, calls=%fused_computation.30 | convolution fusion | flops 1883111424 | bytes 8521728 | tf_op jit(solution)/shard_map/dot_general | solution.py:93
  366.0 0.8 reduce-scatter.7.cloned.1.call-done
  366.8 1.1 copy.49
  368.0 0.1 fusion.35
  368.1 0.8 copy.46
  368.9 0.8 copy.47
  (36 shorter events, 0.2 us)
Async XLA Ops:
  7.2 6.5 %copy-start.12 = (s32[7,4]{0,1:T(4,128)S(1)}, s32[7,4]{0,1:T(4,128)}, u32[]{:S(2)}) copy-start(s32[7,4]{0,1:T(4,128)} %param.17) | copy-start | bytes 340
  7.2 58.8 %copy-start.11 = (f32[512]{0:T(512)S(1)}, f32[512]{0:T(512)}, u32[]{:S(2)}) copy-start(f32[512]{0:T(512)} %param.11) | copy-start | bytes 6148
  7.2 58.5 %all-gather.5.cloned.1.call-start = ((), (), s32[]{:S(2)}) async-start(), calls=%async_computation.2 | async-start | bytes 4456448 | tf_op jit(solution)/shard_map/all_gather | solution.py:39
  9.0 191.3 %reduce-scatter.5.cloned.1.call-start = ((), (), s32[]{:S(2)}) async-start(), calls=%async_computation.3 | async-start | bytes 24772608 | tf_op jit(solution)/shard_map/reduce_scatter | solution.py:58
  66.0 4.2 %copy-start = (bf16[2,2048,512]{2,1,0:T(8,128)(2,1)S(1)}, bf16[2,2048,512]{2,1,0:T(8,128)(2,1)}, u32[]{:S(2)}) copy-start(bf16[2,2048,512]{2,1,0:T(8,128)(2,1)} %all-gather.5.cloned.1.call-done) | copy-start | bytes 12582916
  70.2 2.2 copy-start.2
  70.2 2.5 copy-start.7
  72.7 2.1 copy-start.3
  84.4 0.7 copy-start.15
  84.4 185.5 %all-gather.7.cloned.1.call-start = ((), (), s32[]{:S(2)}) async-start(), calls=%async_computation.4 | async-start | bytes 12386304 | tf_op jit(solution)/shard_map/all_gather | solution.py:81
  204.0 162.8 %reduce-scatter.7.cloned.1.call-start = ((), (), s32[]{:S(2)}) async-start(), calls=%async_computation.5 | async-start | bytes 4456448
  270.0 5.0 %copy-start.4 = (bf16[7,128,4,128]{3,2,1,0:T(4,128)(2,1)S(1)}, bf16[7,128,4,128]{3,2,1,0:T(4,128)(2,1)}, u32[]{:S(2)}) copy-start(bf16[7,128,4,128]{3,2,1,0:T(4,128)(2,1)} %copy-done.3) | copy-start | bytes 2752516
  270.0 5.0 %copy-start.8 = (bf16[896,512]{1,0:T(8,128)(2,1)S(1)}, bf16[896,512]{1,0:T(8,128)(2,1)}, u32[]{:S(2)}) copy-start(bf16[896,512]{1,0:T(8,128)(2,1)} %param.14) | copy-start | bytes 2752516
  270.0 6.1 %copy-start.13 = (bf16[2048,3,896]{0,2,1:T(8,128)(2,1)S(1)}, bf16[2048,3,896]{0,2,1:T(8,128)(2,1)}, u32[]{:S(2)}) copy-start(bf16[2048,3,896]{0,2,1:T(8,128)(2,1)} %all-gather.7.cloned.1.call-done) | copy-start | bytes 33030148
  289.9 0.9 copy-start.9
  289.9 1.0 copy-start.10
  289.9 1.2 copy-start.14
  349.1 5.9 %copy-start.1 = (bf16[2,2048,512]{2,1,0:T(8,128)(2,1)S(1)}, bf16[2,2048,512]{2,1,0:T(8,128)(2,1)}, u32[]{:S(2)}) copy-start(bf16[2,2048,512]{2,1,0:T(8,128)(2,1)} %all-gather.5.cloned.1.call-done) | copy-start | bytes 12582916
  349.2 5.8 %copy-start.5 = (f32[512,896]{1,0:T(8,128)S(1)}, f32[512,896]{1,0:T(8,128)}, u32[]{:S(2)}) copy-start(f32[512,896]{1,0:T(8,128)} %copy.44) | copy-start | bytes 5505028
  355.0 5.6 %copy-start.6 = (f32[512,896]{1,0:T(8,128)S(1)}, f32[512,896]{1,0:T(8,128)}, u32[]{:S(2)}) copy-start(f32[512,896]{1,0:T(8,128)} %copy.42) | copy-start | bytes 5505028
Sparse Core Ops, SparseCore 0:
  10.7 54.8 all-gather.4
  84.6 115.6 reduce-scatter.4
  204.2 65.7 all-gather.6
  290.1 76.6 reduce-scatter.6
where the time goes:
time: 382 us; the launch traced here: 376 us
  waiting for transfers between devices  217 us (57%)
  blocking collectives  64.5 us (17%)
  matrix products  34.7 us (9%)
  local copies, waits for them, and re-layouts  22.1 us (6%)
  other arithmetic  21.6 us (6%)
  between operations  15.4 us (4%)
    reduce_scatter x1, waiting for transfers between devices, shards(): lax.psum_scatter(partial_sums, 'col', scatter_dimension=0, tiled=True)  99 us
    all_gather x1, waiting for transfers between devices, shards(): piece = lax.all_gather(lanes, 'col', axis=0, tiled=True)  65.7 us
    all_gather x1, waiting for transfers between devices, shards(): pieces = lax.all_gather(stacked, 'row', axis=1, tiled=True)  51.9 us
    unnamed x2, blocking collectives  46.6 us
    unnamed x45, local copies, waits for them, and re-layouts  16.3 us
    all_gather x1, blocking collectives, shards(): lax.all_gather(inv_rms, 'col', axis=0, tiled=True)  9.83 us
    concatenate x1, other arithmetic, shards(): partial_sums = jnp.concatenate(products, axis=1)  9.62 us
    all_gather x1, blocking collectives, shards(): lax.all_gather(rms_part, 'col', axis=0, tiled=True)  8.1 us
  transfers between devices with their start and end apart: 4, of which 4 were waited for; matrix products, arithmetic and copies ran while one was open for 8% of the time, Pallas kernels for 0%

commit v1 on v0

v1 whole, which is shorter than its diff:
```python
import jax
import jax.numpy as jnp
from jax import lax
from jax.experimental import pallas as pl
from jax.experimental.pallas import tpu as pltpu
from jax.sharding import PartitionSpec as P

epsilon = 1e-05
MESH = pl.DeviceIdType.MESH
BF = jnp.bfloat16
F32 = jnp.float32

CHUNKS = 4
TOK = 16
HALF = 64
WIDE = 512
CHIP = 1024
FF = 896
GU = 2 * FF
ALL = 3 * FF
MODEL = 4096


def mm(a, b):
    return jnp.dot(a, b, preferred_element_type=F32)


def mm_nt(a, b):
    return lax.dot_general(a, b, (((1,), (1,)), ((), ())), preferred_element_type=F32)


def body(
    tok_ref, cot_ref, gain_ref, gw_ref, uw_ref, dw_ref, gm_ref, um_ref, dm_ref,
    mixed_ref, ig_ref, gg_ref, ug_ref, dg_ref,
    tokb, cotb, gain8, gainb, ssq, invb, rmsb, gath, wgu, wd, part, rel, full, hid, outp, rs1, sum1, rs2,
    fw, bw, acc_gu, acc_d, xt, ht, send_gu, send_d, recv_gu, recv_d, mixb, igb,
    sw_s, sw_r, sq_s, sq_r, p1_s, p1_r, p2_s, p2_r, r_s, r_r, f_s, f_r, g_s, g_r, h_s, h_r,
    a_s, a_r, b_s, b_r, w_s, w_r, m_s, m_r, o_s, o_r,
):
    row = lax.axis_index("row")
    col = lax.axis_index("col")
    z, x, y, c = row // 4, row % 4, col // 2, col % 2
    other = 1 - c
    up, dn, op = (y + 1) % 4, (y + 3) % 4, (y + 2) % 4

    def dev(dz, dx, dy, dc):
        return (dz * 4 + dx, dy * 2 + dc)

    twin = dev(z, x, y, other)
    up_dev, dn_dev = dev(z, x, up, c), dev(z, x, dn, c)

    def zdev(j):
        return dev((z + j) % 4, x, y, c)

    def xdev(j):
        return dev(z, (x + j) % 4, y, c)

    def ydev(j):
        return dev(z, x, (y + j) % 4, c)

    def rc(src, dst, ss, rs, to):
        return pltpu.make_async_remote_copy(
            src_ref=src, dst_ref=dst, send_sem=ss, recv_sem=rs, device_id=to, device_id_type=MESH
        )

    def start(copies):
        for copy in copies:
            copy.start()

    def finish(copies):
        for copy in copies:
            copy.wait()

    lo = pl.ds(0, CHIP)
    hi = pl.ds(CHIP, CHIP)
    mine = pl.ds(pl.multiple_of(c * WIDE, WIDE), WIDE)
    theirs = pl.ds(pl.multiple_of(other * WIDE, WIDE), WIDE)
    my_rows = pl.ds(pl.multiple_of(c * HALF, HALF), HALF)
    their_rows = pl.ds(pl.multiple_of(other * HALF, HALF), HALF)

    barrier = pltpu.get_barrier_semaphore()
    peers = [twin] + [f(j) for f in (xdev, ydev, zdev) for j in (1, 2, 3)]
    for peer in peers:
        pl.semaphore_signal(barrier, inc=1, device_id=peer, device_id_type=MESH)

    @pl.loop(0, 4)
    def _(i):
        rows = pl.ds(pl.multiple_of(i * 128, 128), 128)
        to = pl.ds(pl.multiple_of(c * WIDE + i * 128, 128), 128)
        for j in range(7):
            cols = slice(j * 128, j * 128 + 128)
            keep = gm_ref[i, j].astype(F32)
            wgu[to, j * 128 : j * 128 + 128] = (gw_ref[rows, cols].astype(F32) * keep).astype(BF)
            keep = um_ref[i, j].astype(F32)
            wgu[to, FF + j * 128 : FF + j * 128 + 128] = (uw_ref[rows, cols].astype(F32) * keep).astype(BF)

    @pl.loop(0, 7)
    def _(i):
        rows = pl.ds(pl.multiple_of(i * 128, 128), 128)
        for j in range(4):
            to = pl.ds(pl.multiple_of(c * WIDE + j * 128, 128), 128)
            keep = dm_ref[i, j].astype(F32)
            wd[rows, to] = (dw_ref[rows, j * 128 : j * 128 + 128].astype(F32) * keep).astype(BF)

    gain8[...] = jnp.broadcast_to(gain_ref[...], (8, WIDE))
    tokb[:, mine] = tok_ref[my_rows, :]
    cotb[:, mine] = cot_ref[my_rows, :]
    gainb[:, mine] = gain8[...]

    pl.semaphore_wait(barrier, len(peers))

    swaps = [
        rc(cot_ref.at[their_rows, :], cotb.at[:, mine], sw_s.at[0], sw_r.at[0], twin),
        rc(tok_ref.at[their_rows, :], tokb.at[:, mine], sw_s.at[1], sw_r.at[1], twin),
        rc(gain8, gainb.at[:, mine], sw_s.at[2], sw_r.at[2], twin),
        rc(wd.at[:, mine], wd.at[:, mine], sw_s.at[3], sw_r.at[3], twin),
        rc(wgu.at[mine, :], wgu.at[mine, :], sw_s.at[4], sw_r.at[4], twin),
    ]
    start(swaps)

    def gather_x(k):
        return [
            rc(gath.at[k, z, x, :, lo], gath.at[k, z, x, :, lo], p1_s.at[k, 0, j - 1], p1_r.at[k, 0, j - 1], xdev(j))
            for j in (1, 2, 3)
        ]

    def gather_z(k):
        return [
            rc(gath.at[k, z, x, :, hi], gath.at[k, z, x, :, hi], p1_s.at[k, 1, j - 1], p1_r.at[k, 1, j - 1], zdev(j))
            for j in (1, 2, 3)
        ]

    def gather_rest(k):
        return [
            rc(gath.at[k, z, :, :, lo], gath.at[k, z, :, :, lo], p2_s.at[k, 0, j - 1], p2_r.at[k, 0, j - 1], zdev(j))
            for j in (1, 2, 3)
        ] + [
            rc(gath.at[k, :, x, :, hi], gath.at[k, :, x, :, hi], p2_s.at[k, 1, j - 1], p2_r.at[k, 1, j - 1], xdev(j))
            for j in (1, 2, 3)
        ]

    finish(swaps[0:1])
    for k in range(CHUNKS):
        gath[k, z, x, :, hi] = cotb[k * TOK : (k + 1) * TOK, :]
    start(gather_z(0))

    finish(swaps[1:3])
    tok = tokb[...].astype(F32)
    ssq[y] = jnp.broadcast_to(jnp.sum(tok * tok, axis=1, keepdims=True), (HALF, 128))
    sends = [rc(ssq.at[y], ssq.at[y], sq_s.at[j - 1], sq_r.at[j - 1], ydev(j)) for j in (1, 2, 3)]
    start(sends)
    finish(sends)
    invb[...] = 1.0 / jnp.sqrt((ssq[0] + ssq[1] + ssq[2] + ssq[3]) / MODEL + epsilon)
    for k in range(CHUNKS):
        rows = slice(k * TOK, (k + 1) * TOK)
        scaled = tokb[rows, :].astype(F32) * gainb[0:1, :] * invb[rows, 0:1]
        gath[k, z, x, :, lo] = scaled.astype(BF)
    start(gather_x(0))

    @pl.loop(0, 16)
    def _(i):
        acc_gu[pl.ds(pl.multiple_of(i * 64, 64), 64), :] = jnp.zeros((64, GU), F32)
        acc_d[pl.ds(pl.multiple_of(i * 56, 56), 56), :] = jnp.zeros((56, CHIP), F32)

    finish(gather_z(0))
    finish(gather_x(0))
    start(gather_rest(0))
    start(gather_x(1) + gather_z(1))
    finish(swaps[3:5])

    def relay(k, s):
        return [
            rc(part.at[s, op, pl.ds(0, 32), :], rel.at[k, 0], r_s.at[k, 0], r_r.at[k, 0], up_dev),
            rc(part.at[s, op, pl.ds(32, 32), :], rel.at[k, 1], r_s.at[k, 1], r_r.at[k, 1], dn_dev),
        ]

    def quarter(k, s):
        return [
            rc(part.at[s, up], full.at[k, 0], f_s.at[k, 0], f_r.at[k, 0], up_dev),
            rc(part.at[s, dn], full.at[k, 1], f_s.at[k, 1], f_r.at[k, 1], dn_dev),
        ]

    def share(k):
        return [
            rc(hid.at[k, y], hid.at[k, y], g_s.at[k, 0], g_r.at[k, 0], up_dev),
            rc(hid.at[k, y], hid.at[k, y], g_s.at[k, 1], g_r.at[k, 1], dn_dev),
        ]

    def pass_on(k):
        first = hid.at[k, dn, pl.ds(0, 32), :]
        second = hid.at[k, up, pl.ds(32, 32), :]
        return [
            rc(first, first, h_s.at[k, 0], h_r.at[k, 0], up_dev),
            rc(second, second, h_s.at[k, 1], h_r.at[k, 1], dn_dev),
        ]

    def scatter(k, s):
        return [
            rc(outp.at[s, :, (x + j) % 4, :, lo], rs1.at[k, 0, j - 1], a_s.at[k, 0, j - 1], a_r.at[k, 0, j - 1], xdev(j))
            for j in (1, 2, 3)
        ] + [
            rc(outp.at[s, (z + j) % 4, :, :, hi], rs1.at[k, 1, j - 1], a_s.at[k, 1, j - 1], a_r.at[k, 1, j - 1], zdev(j))
            for j in (1, 2, 3)
        ]

    def scatter_rest(k):
        return [
            rc(sum1.at[k, 0, (z + j) % 4], rs2.at[k, 0, j - 1], b_s.at[k, 0, j - 1], b_r.at[k, 0, j - 1], zdev(j))
            for j in (1, 2, 3)
        ] + [
            rc(sum1.at[k, 1, (x + j) % 4], rs2.at[k, 1, j - 1], b_s.at[k, 1, j - 1], b_r.at[k, 1, j - 1], xdev(j))
            for j in (1, 2, 3)
        ]

    def project(k):
        s = k % 2

        @pl.loop(0, 7)
        def _(n):
            cols = pl.ds(pl.multiple_of(n * 256, 256), 256)
            got = mm(gath[k, :, :, :, lo].reshape(256, CHIP), wgu[:, cols])
            part[s, :, :, cols] = got.astype(BF).reshape(4, 64, 256)

        for n, wide in ((0, 256), (256, 256), (512, 256), (768, 128)):
            got = mm_nt(gath[k, :, :, :, hi].reshape(256, CHIP), wd[n : n + wide, :])
            part[s, :, :, GU + n : GU + n + wide] = got.astype(BF).reshape(4, 64, wide)

    def add_relay(k):
        s = k % 2

        @pl.loop(0, 7)
        def _(n):
            cols = pl.ds(pl.multiple_of(n * 384, 128), 384)
            part[s, up, 0:32, cols] = (part[s, up, 0:32, cols].astype(F32) + rel[k, 0, :, cols].astype(F32)).astype(BF)
            part[s, dn, 32:64, cols] = (part[s, dn, 32:64, cols].astype(F32) + rel[k, 1, :, cols].astype(F32)).astype(BF)

    def activate(k):
        s = k % 2

        @pl.loop(0, 7)
        def _(n):
            def total(base):
                cols = pl.ds(pl.multiple_of(base + n * 128, 128), 128)
                return part[s, y, :, cols].astype(F32) + full[k, 0, :, cols].astype(F32) + full[k, 1, :, cols].astype(F32)

            gate, up_value, back = total(0), total(FF), total(GU)
            sigma = jax.nn.sigmoid(gate)
            activ = gate * sigma
            d_gate = back * up_value * sigma * (1.0 + gate * (1.0 - sigma))
            hid[k, y, :, pl.ds(pl.multiple_of(n * 128, 128), 128)] = (activ * up_value).astype(BF)
            hid[k, y, :, pl.ds(pl.multiple_of(FF + n * 128, 128), 128)] = d_gate.astype(BF)
            hid[k, y, :, pl.ds(pl.multiple_of(GU + n * 128, 128), 128)] = (back * activ).astype(BF)

    def products(k):
        s = k % 2

        @pl.loop(0, 4)
        def _(n):
            cols = pl.ds(pl.multiple_of(n * 256, 256), 256)
            got = mm(hid[k, :, :, 0:FF].reshape(256, FF), wd[:, cols])
            outp[s, :, :, :, cols] = got.astype(BF).reshape(4, 4, TOK, 256)
            got = mm_nt(hid[k, :, :, FF:ALL].reshape(256, GU), wgu[cols, :])
            outp[s, :, :, :, pl.ds(pl.multiple_of(CHIP + n * 256, 256), 256)] = got.astype(BF).reshape(4, 4, TOK, 256)

    def weight_sums(k):
        xt[...] = gath[k, :, :, :, lo].reshape(256, CHIP).T
        ht[...] = hid[k, :, :, 0:FF].reshape(256, FF).T

        @pl.loop(0, 7)
        def _(n):
            cols = pl.ds(pl.multiple_of(n * 256, 256), 256)
            from_cols = pl.ds(pl.multiple_of(FF + n * 256, 128), 256)
            pulled = hid[k, :, :, from_cols].reshape(256, 256)
            for m in range(4):
                acc_gu[m * 256 : m * 256 + 256, cols] += mm(xt[m * 256 : m * 256 + 256, :], pulled)

        @pl.loop(0, 4)
        def _(n):
            cols = pl.ds(pl.multiple_of(n * 256, 256), 256)
            from_cols = pl.ds(pl.multiple_of(CHIP + n * 256, 256), 256)
            cots = gath[k, :, :, :, from_cols].reshape(256, 256)
            for m, high in ((0, 256), (256, 256), (512, 256), (768, 128)):
                acc_d[m : m + high, cols] += mm(ht[m : m + high, :], cots)

    def sum_first(k):
        s = k % 2
        for i in range(4):
            total = outp[s, i, x, :, lo].astype(F32)
            for j in range(3):
                total += rs1[k, 0, j, i].astype(F32)
            sum1[k, 0, i] = total.astype(BF)
            total = outp[s, z, i, :, hi].astype(F32)
            for j in range(3):
                total += rs1[k, 1, j, i].astype(F32)
            sum1[k, 1, i] = total.astype(BF)

    def sum_last(k):
        rows = pl.ds(pl.multiple_of(k * TOK, TOK), TOK)
        total = sum1[k, 0, z].astype(F32)
        for j in range(3):
            total += rs2[k, 0, j].astype(F32)
        fw[rows, :] = total
        total = sum1[k, 1, x].astype(F32)
        for j in range(3):
            total += rs2[k, 1, j].astype(F32)
        bw[rows, :] = total

    exchange = [
        rc(send_gu, recv_gu, w_s.at[0], w_r.at[0], twin),
        rc(send_d, recv_d, w_s.at[1], w_r.at[1], twin),
    ]

    def step(i, carry):
        def at(k):
            return jnp.logical_and(k >= 0, k < CHUNKS)

        @pl.when(at(i - 2))
        def _():
            k = i - 2
            finish(quarter(k, k % 2))
            activate(k)
            start(share(k))

        @pl.when(at(i - 1))
        def _():
            k = i - 1
            finish(relay(k, k % 2))
            add_relay(k)
            start(quarter(k, k % 2))

        @pl.when(i + 1 < CHUNKS)
        def _():
            finish(gather_x(i + 1) + gather_z(i + 1))
            start(gather_rest(i + 1))

        @pl.when(i + 2 < CHUNKS)
        def _():
            start(gather_x(i + 2) + gather_z(i + 2))

        @pl.when(i < CHUNKS)
        def _():
            finish(gather_rest(i))
            project(i)
            start(relay(i, i % 2))

        @pl.when(at(i - 4))
        def _():
            k = i - 4
            finish(scatter(k, k % 2))
            sum_first(k)
            start(scatter_rest(k))

        @pl.when(at(i - 3))
        def _():
            k = i - 3
            finish(pass_on(k))
            products(k)
            start(scatter(k, k % 2))
            weight_sums(k)

        @pl.when(i - 3 == CHUNKS - 1)
        def _():
            @pl.loop(0, 4)
            def _(n):
                rows = pl.ds(pl.multiple_of(n * 128, 128), 128)
                src = pl.ds(pl.multiple_of(other * WIDE + n * 128, 128), 128)
                send_gu[rows, :] = acc_gu[src, :].astype(BF)

            send_d[...] = acc_d[:, theirs].astype(BF)
            start(exchange)

        @pl.when(at(i - 5))
        def _():
            k = i - 5
            finish(scatter_rest(k))
            sum_last(k)

        @pl.when(at(i - 2))
        def _():
            k = i - 2
            finish(share(k))
            start(pass_on(k))

        return carry

    lax.fori_loop(0, CHUNKS + 5, step, 0)

    pull = jnp.sum(tokb[...].astype(F32) * gainb[0:1, :] * bw[...], axis=1, keepdims=True)
    rmsb[y] = jnp.broadcast_to(pull, (HALF, 128)) * invb[...]
    sends = [rc(rmsb.at[y], rmsb.at[y], m_s.at[j - 1], m_r.at[j - 1], ydev(j)) for j in (1, 2, 3)]
    start(sends)
    mixb[...] = (tokb[...].astype(F32) + fw[...]).astype(BF)
    mixed_ref[my_rows, :] = mixb[:, mine]
    back = [rc(mixb.at[:, theirs], mixed_ref.at[my_rows, :], o_s.at[0], o_r.at[0], twin)]
    start(back)
    finish(sends)
    inv = invb[:, 0:1]
    fix = inv * inv * ((rmsb[0] + rmsb[1]) + (rmsb[2] + rmsb[3]))[:, 0:1] / MODEL
    igb[...] = (
        cotb[...].astype(F32) + gainb[0:1, :] * (inv * bw[...]) - tokb[...].astype(F32) * fix
    ).astype(BF)
    ig_ref[my_rows, :] = igb[:, mine]
    back += [rc(igb.at[:, theirs], ig_ref.at[my_rows, :], o_s.at[1], o_r.at[1], twin)]
    start(back[1:])

    finish(exchange)

    @pl.loop(0, 4)
    def _(i):
        rows = pl.ds(pl.multiple_of(i * 128, 128), 128)
        src = pl.ds(pl.multiple_of(c * WIDE + i * 128, 128), 128)
        for j in range(7):
            cols = slice(j * 128, j * 128 + 128)
            wide = slice(FF + j * 128, FF + j * 128 + 128)
            total = acc_gu[src, cols] + recv_gu[rows, cols].astype(F32)
            gg_ref[rows, cols] = (total * gm_ref[i, j].astype(F32)).astype(BF)
            total = acc_gu[src, wide] + recv_gu[rows, wide].astype(F32)
            ug_ref[rows, cols] = (total * um_ref[i, j].astype(F32)).astype(BF)

    @pl.loop(0, 7)
    def _(i):
        rows = pl.ds(pl.multiple_of(i * 128, 128), 128)
        for j in range(4):
            cols = slice(j * 128, j * 128 + 128)
            src = pl.ds(pl.multiple_of(c * WIDE + j * 128, 128), 128)
            total = acc_d[rows, src] + recv_d[rows, cols].astype(F32)
            dg_ref[rows, cols] = (total * dm_ref[i, j].astype(F32)).astype(BF)

    finish(back)


def shards(tokens, cotangent, norm_gain, gate_w, up_w, down_w, gate_b, up_b, down_b):
    vmem = pl.BlockSpec(memory_space=pltpu.VMEM)
    smem = pl.BlockSpec(memory_space=pltpu.SMEM)

    def dma(*shape):
        return [pltpu.SemaphoreType.DMA(shape)] * 2

    V = pltpu.VMEM
    out = jax.ShapeDtypeStruct
    return pl.pallas_call(
        body,
        out_shape=(
            out(tokens.shape, BF),
            out(tokens.shape, BF),
            out(gate_w.shape, BF),
            out(up_w.shape, BF),
            out(down_w.shape, BF),
        ),
        in_specs=[vmem] * 6 + [smem] * 3,
        out_specs=(vmem,) * 5,
        scratch_shapes=[
            V((HALF, CHIP), BF),
            V((HALF, CHIP), BF),
            V((8, WIDE), F32),
            V((8, CHIP), F32),
            V((4, HALF, 128), F32),
            V((HALF, 128), F32),
            V((4, HALF, 128), F32),
            V((CHUNKS, 4, 4, TOK, 2 * CHIP), BF),
            V((CHIP, GU), BF),
            V((FF, CHIP), BF),
            V((2, 4, 64, ALL), BF),
            V((CHUNKS, 2, 32, ALL), BF),
            V((CHUNKS, 2, 64, ALL), BF),
            V((CHUNKS, 4, 64, ALL), BF),
            V((2, 4, 4, TOK, 2 * CHIP), BF),
            V((CHUNKS, 2, 3, 4, TOK, CHIP), BF),
            V((CHUNKS, 2, 4, TOK, CHIP), BF),
            V((CHUNKS, 2, 3, TOK, CHIP), BF),
            V((HALF, CHIP), F32),
            V((HALF, CHIP), F32),
            V((CHIP, GU), F32),
            V((FF, CHIP), F32),
            V((CHIP, 256), BF),
            V((FF, 256), BF),
            V((WIDE, GU), BF),
            V((FF, WIDE), BF),
            V((WIDE, GU), BF),
            V((FF, WIDE), BF),
            V((HALF, CHIP), BF),
            V((HALF, CHIP), BF),
        ]
        + dma(5)
        + dma(3)
        + dma(CHUNKS, 2, 3)
        + dma(CHUNKS, 2, 3)
        + dma(CHUNKS, 2)
        + dma(CHUNKS, 2)
        + dma(CHUNKS, 2)
        + dma(CHUNKS, 2)
        + dma(CHUNKS, 2, 3)
        + dma(CHUNKS, 2, 3)
        + dma(2)
        + dma(3)
        + dma(2),
        compiler_params=pltpu.CompilerParams(
            collective_id=0, has_side_effects=True, vmem_limit_bytes=62 * 1024 * 1024
        ),
        cost_estimate=pl.CostEstimate(flops=17_000_000_000, bytes_accessed=6_000_000, transcendentals=2_000_000),
        name="ffn",
    )(tokens, cotangent, norm_gain.reshape(1, -1), gate_w, up_w, down_w, gate_b, up_b, down_b)


def solution(mesh):
    in_specs = (
        P("row", "col"),
        P("row", "col"),
        P("col"),
        P("col", "row"),
        P("col", "row"),
        P("row", "col"),
        P("col", "row"),
        P("col", "row"),
        P("row", "col"),
    )
    out_specs = (
        P("row", "col"),
        P("row", "col"),
        P("col", "row"),
        P("col", "row"),
        P("row", "col"),
    )
    return jax.shard_map(shards, mesh=mesh, in_specs=in_specs, out_specs=out_specs, check_vma=False)
```

time: 382 us -> 156 us (0.41); the launches traced: 376 us -> 156 us
  waiting for transfers between devices: 217 us -> 0 us
  Pallas kernels: 0 us -> 147 us
  blocking collectives: 64.5 us -> 0 us
  matrix products: 34.7 us -> 0 us
  other arithmetic: 21.6 us -> 0 us
  between operations: 15.4 us -> 0.65 us
  local copies, waits for them, and re-layouts: 22.1 us -> 8.31 us
    pallas_call x0 -> x1, Pallas kernels: none -> 147 us  [shards(): pl.pallas_call(body, out_shape=(out(tokens.shape, BF), out(tokens.shape,...]
    all_gather x2 -> x0, waiting for transfers between devices: 118 us -> none  [the longest x1 65.7 us: shards(): piece = lax.all_gather(lanes, 'col', axis=0, tiled=True)]
    reduce_scatter x1 -> x0, waiting for transfers between devices: 99 us -> none  [shards(): lax.psum_scatter(partial_sums, 'col', scatter_dimension=0, tiled=True)]
    unnamed x2 -> x0, blocking collectives: 46.6 us -> none
    dot_general x9 -> x0, matrix products: 34.7 us -> none  [the longest x1 5.83 us: shards(): lax.dot_general(hidden_piece, cot_all, contract, preferred_element_type=j...]
    all_gather x2 -> x0, blocking collectives: 17.9 us -> none  [the longest x1 9.83 us: shards(): lax.all_gather(inv_rms, 'col', axis=0, tiled=True)]
    concatenate x2 -> x0, other arithmetic: 12.2 us -> none  [the longest x1 9.62 us: shards(): partial_sums = jnp.concatenate(products, axis=1)]
    unnamed x45 -> x12, local copies, waits for them, and re-layouts: 16.3 us -> 8.31 us
  transfers between devices with their start and end apart: 4 -> 0, of which waited for: 4 -> 0; matrix products, arithmetic and copies ran while one was open for 8% -> 0% of each run, Pallas kernels for 0% -> 0%
where the time goes in v1:
time: 156 us
  Pallas kernels  147 us (94%)
  local copies, waits for them, and re-layouts  8.31 us (5%)
    pallas_call x1, Pallas kernels, shards(): pl.pallas_call(body, out_shape=(out(tokens.shape, BF), out(tokens.shape,...  147 us
    unnamed x12, local copies, waits for them, and re-layouts  8.31 us

profile of v1, /device:TPU:1, one launch (start us, length us, event | category | flops | bytes accessed | tf_op | source)
XLA Modules:
  0.0 155.8 jit_solution(4507649981546385133)
XLA Ops:
  0.6 1.4 copy.14.dm_ref
  2.0 146.8 %ffn.1 = (bf16[128,512]{1,0:T(8,128)(2,1)}, bf16[128,512]{1,0:T(8,128)(2,1)}, bf16[512,896]{1,0:T(8,128)(2,1)}, bf16[512,896]{1,0:T(8,128)(2,1)}, bf16[896,512]{1,0:T(8,128)(2,1)}) custom-call(bf16[128,512]{1,0:T(8,128)(2,1)} %tok_ref.1, bf16[128,512]{1,0:T(8,128)(2,1)} %cot_ref.1, f32[1,512]{1,0:T(1,128)} %bitcast.1, bf16[512,896]{1,0:T(8,128)(2,1)} %gw_ref.1, ...), custom_call_target="tpu_custom_call" | custom-call | flops 16999999488 | bytes 6000000 | tf_op jit(solution)/shard_map/ffn/pallas_call | solution.py:441
  148.8 0.0 copy-start.2
  148.8 1.6 %copy.20 = bf16[128,512]{1,0:T(8,128)(2,1)} copy(bf16[128,512]{1,0:T(8,128)(2,1)} %get-tuple-element.10) | data formatting | bytes 262144
  150.4 0.0 copy-done.2
  150.4 0.7 copy.21
  151.1 0.0 copy-start.1
  151.1 2.3 %copy.22 = bf16[512,896]{1,0:T(8,128)(2,1)} copy(bf16[512,896]{1,0:T(8,128)(2,1)} %get-tuple-element.12) | data formatting | bytes 1835008
  153.3 0.0 copy-done.1
  153.3 0.0 copy-start
  153.3 0.9 copy.23
  154.3 0.6 copy-done
  154.8 0.9 copy.24
Async XLA Ops:
  148.8 1.6 %copy-start.2 = (bf16[128,512]{1,0:T(8,128)(2,1)S(1)}, bf16[128,512]{1,0:T(8,128)(2,1)}, u32[]{:S(2)}) copy-start(bf16[128,512]{1,0:T(8,128)(2,1)} %get-tuple-element.11) | copy-start | bytes 393220
  151.1 2.3 %copy-start.1 = (bf16[512,896]{1,0:T(8,128)(2,1)S(1)}, bf16[512,896]{1,0:T(8,128)(2,1)}, u32[]{:S(2)}) copy-start(bf16[512,896]{1,0:T(8,128)(2,1)} %get-tuple-element.13) | copy-start | bytes 2752516
  153.3 1.5 copy-start

commit v2 on v1

--- a/solution.py
+++ b/solution.py
@@ -73,6 +73,19 @@
 
     lo = pl.ds(0, CHIP)
     hi = pl.ds(CHIP, CHIP)
+
+    def strip(a, h):
+        return pl.ds(a * CHIP + h * WIDE, WIDE)
+
+    spot = lax.broadcasted_iota(jnp.int32, (HALF, 128), 0) == lax.broadcasted_iota(jnp.int32, (HALF, 128), 1)
+
+    def to_lanes(column):
+        line = jnp.sum(jnp.where(spot, jnp.broadcast_to(column, (HALF, 128)), 0.0), axis=0, keepdims=True)
+        return jnp.broadcast_to(line, (8, 128))
+
+    def to_column(line):
+        return jnp.sum(jnp.where(spot, jnp.broadcast_to(line, (HALF, 128)), 0.0), axis=1, keepdims=True)
+
     mine = pl.ds(pl.multiple_of(c * WIDE, WIDE), WIDE)
     theirs = pl.ds(pl.multiple_of(other * WIDE, WIDE), WIDE)
     my_rows = pl.ds(pl.multiple_of(c * HALF, HALF), HALF)
@@ -99,7 +112,7 @@
         rows = pl.ds(pl.multiple_of(i * 128, 128), 128)
         for j in range(4):
             to = pl.ds(pl.multiple_of(c * WIDE + j * 128, 128), 128)
-            keep = dm_ref[i, j].astype(F32)
+            keep = dm_ref[j, i].astype(F32)
             wd[rows, to] = (dw_ref[rows, j * 128 : j * 128 + 128].astype(F32) * keep).astype(BF)
 
     gain8[...] = jnp.broadcast_to(gain_ref[...], (8, WIDE))
@@ -118,72 +131,74 @@
     ]
     start(swaps)
 
-    def gather_x(k):
-        return [
-            rc(gath.at[k, z, x, :, lo], gath.at[k, z, x, :, lo], p1_s.at[k, 0, j - 1], p1_r.at[k, 0, j - 1], xdev(j))
-            for j in (1, 2, 3)
-        ]
-
-    def gather_z(k):
-        return [
-            rc(gath.at[k, z, x, :, hi], gath.at[k, z, x, :, hi], p1_s.at[k, 1, j - 1], p1_r.at[k, 1, j - 1], zdev(j))
-            for j in (1, 2, 3)
-        ]
-
-    def gather_rest(k):
-        return [
-            rc(gath.at[k, z, :, :, lo], gath.at[k, z, :, :, lo], p2_s.at[k, 0, j - 1], p2_r.at[k, 0, j - 1], zdev(j))
-            for j in (1, 2, 3)
-        ] + [
-            rc(gath.at[k, :, x, :, hi], gath.at[k, :, x, :, hi], p2_s.at[k, 1, j - 1], p2_r.at[k, 1, j - 1], xdev(j))
-            for j in (1, 2, 3)
-        ]
+    def near(k, a):
+        def one(h, to, j):
+            block = gath.at[k, z, x, :, strip(a, h)]
+            return rc(block, block, p1_s.at[k, a, h, j - 1], p1_r.at[k, a, h, j - 1], to(j))
+
+        return [one(h, to, j) for j in (1, 2, 3) for h, to in ((0, xdev), (1, zdev))]
+
+    def rest(k, a):
+        def one(h, to, j):
+            block = gath.at[k, z, :, :, strip(a, 0)] if h == 0 else gath.at[k, :, x, :, strip(a, 1)]
+            return rc(block, block, p2_s.at[k, a, h, j - 1], p2_r.at[k, a, h, j - 1], to(j))
+
+        return [one(h, to, j) for j in (1, 2, 3) for h, to in ((0, zdev), (1, xdev))]
 
     finish(swaps[0:1])
     for k in range(CHUNKS):
         gath[k, z, x, :, hi] = cotb[k * TOK : (k + 1) * TOK, :]
-    start(gather_z(0))
+    start(near(0, 1))
 
     finish(swaps[1:3])
     tok = tokb[...].astype(F32)
-    ssq[y] = jnp.broadcast_to(jnp.sum(tok * tok, axis=1, keepdims=True), (HALF, 128))
+    ssq[y] = to_lanes(jnp.sum(tok * tok, axis=1, keepdims=True))
     sends = [rc(ssq.at[y], ssq.at[y], sq_s.at[j - 1], sq_r.at[j - 1], ydev(j)) for j in (1, 2, 3)]
     start(sends)
+    finish(near(0, 1))
+    start(rest(0, 1))
     finish(sends)
-    invb[...] = 1.0 / jnp.sqrt((ssq[0] + ssq[1] + ssq[2] + ssq[3]) / MODEL + epsilon)
+    squares = to_column(((ssq[0] + ssq[1]) + (ssq[2] + ssq[3]))[0:1, :])
+    invb[...] = jnp.broadcast_to(1.0 / jnp.sqrt(squares / MODEL + epsilon), (HALF, 128))
     for k in range(CHUNKS):
         rows = slice(k * TOK, (k + 1) * TOK)
         scaled = tokb[rows, :].astype(F32) * gainb[0:1, :] * invb[rows, 0:1]
         gath[k, z, x, :, lo] = scaled.astype(BF)
-    start(gather_x(0))
+    start(near(0, 0))
 
     @pl.loop(0, 16)
     def _(i):
         acc_gu[pl.ds(pl.multiple_of(i * 64, 64), 64), :] = jnp.zeros((64, GU), F32)
         acc_d[pl.ds(pl.multiple_of(i * 56, 56), 56), :] = jnp.zeros((56, CHIP), F32)
 
-    finish(gather_z(0))
-    finish(gather_x(0))
-    start(gather_rest(0))
-    start(gather_x(1) + gather_z(1))
+    finish(near(0, 0))
+    start(rest(0, 0))
+    start(near(1, 1) + near(1, 0))
     finish(swaps[3:5])
 
-    def relay(k, s):
+    def span(a):
+        return pl.ds(GU, FF) if a == 1 else pl.ds(0, GU)
+
+    def relay(k, s, a):
+        one = part.at[s, op, pl.ds(0, 32), span(a)]
+        two = part.at[s, op, pl.ds(32, 32), span(a)]
         return [
-            rc(part.at[s, op, pl.ds(0, 32), :], rel.at[k, 0], r_s.at[k, 0], r_r.at[k, 0], up_dev),
-            rc(part.at[s, op, pl.ds(32, 32), :], rel.at[k, 1], r_s.at[k, 1], r_r.at[k, 1], dn_dev),
+            rc(one, rel.at[k, 0, :, span(a)], r_s.at[k, a, 0], r_r.at[k, a, 0], up_dev),
+            rc(two, rel.at[k, 1, :, span(a)], r_s.at[k, a, 1], r_r.at[k, a, 1], dn_dev),
         ]
 
-    def quarter(k, s):
+    def quarter(k, s, a):
         return [
-            rc(part.at[s, up], full.at[k, 0], f_s.at[k, 0], f_r.at[k, 0], up_dev),
-            rc(part.at[s, dn], full.at[k, 1], f_s.at[k, 1], f_r.at[k, 1], dn_dev),
+            rc(part.at[s, up, :, span(a)], full.at[k, 0, :, span(a)], f_s.at[k, a, 0], f_r.at[k, a, 0], up_dev),
+            rc(part.at[s, dn, :, span(a)], full.at[k, 1, :, span(a)], f_s.at[k, a, 1], f_r.at[k, a, 1], dn_dev),
         ]
 
-    def share(k):
+    def share(k, later):
+        one = hid.at[k, y, pl.ds(32 if later else 0, 32), :]
+        two = hid.at[k, y, pl.ds(0 if later else 32, 32), :]
         return [
-            rc(hid.at[k, y], hid.at[k, y], g_s.at[k, 0], g_r.at[k, 0], up_dev),
-            rc(hid.at[k, y], hid.at[k, y], g_s.at[k, 1], g_r.at[k, 1], dn_dev),
+            rc(one, one, g_s.at[k, later, 0], g_r.at[k, later, 0], up_dev),
+            rc(two, two, g_s.at[k, later, 1], g_r.at[k, later, 1], dn_dev),
         ]
 
     def pass_on(k):
@@ -194,25 +209,21 @@
             rc(second, second, h_s.at[k, 1], h_r.at[k, 1], dn_dev),
         ]
 
-    def scatter(k, s):
-        return [
-            rc(outp.at[s, :, (x + j) % 4, :, lo], rs1.at[k, 0, j - 1], a_s.at[k, 0, j - 1], a_r.at[k, 0, j - 1], xdev(j))
-            for j in (1, 2, 3)
-        ] + [
-            rc(outp.at[s, (z + j) % 4, :, :, hi], rs1.at[k, 1, j - 1], a_s.at[k, 1, j - 1], a_r.at[k, 1, j - 1], zdev(j))
-            for j in (1, 2, 3)
-        ]
-
-    def scatter_rest(k):
-        return [
-            rc(sum1.at[k, 0, (z + j) % 4], rs2.at[k, 0, j - 1], b_s.at[k, 0, j - 1], b_r.at[k, 0, j - 1], zdev(j))
-            for j in (1, 2, 3)
-        ] + [
-            rc(sum1.at[k, 1, (x + j) % 4], rs2.at[k, 1, j - 1], b_s.at[k, 1, j - 1], b_r.at[k, 1, j - 1], xdev(j))
-            for j in (1, 2, 3)
-        ]
-
-    def project(k):
+    def scatter(k, s, a):
+        def one(h, to, j):
+            block = outp.at[s, :, (x + j) % 4, :, strip(a, 0)] if h == 0 else outp.at[s, (z + j) % 4, :, :, strip(a, 1)]
+            return rc(block, rs1.at[k, a, h, j - 1], a_s.at[k, a, h, j - 1], a_r.at[k, a, h, j - 1], to(j))
+
+        return [one(h, to, j) for j in (1, 2, 3) for h, to in ((0, xdev), (1, zdev))]
+
+    def scatter_rest(k, a):
+        def one(h, to, j):
+            block = sum1.at[k, a, h, ((z if h == 0 else x) + j) % 4]
+            return rc(block, rs2.at[k, a, h, j - 1], b_s.at[k, a, h, j - 1], b_r.at[k, a, h, j - 1], to(j))
+
+        return [one(h, to, j) for j in (1, 2, 3) for h, to in ((0, zdev), (1, xdev))]
+
+    def project_pre(k):
         s = k % 2
 
         @pl.loop(0, 7)
@@ -221,16 +232,19 @@
             got = mm(gath[k, :, :, :, lo].reshape(256, CHIP), wgu[:, cols])
             part[s, :, :, cols] = got.astype(BF).reshape(4, 64, 256)
 
+    def project_back(k):
+        s = k % 2
         for n, wide in ((0, 256), (256, 256), (512, 256), (768, 128)):
             got = mm_nt(gath[k, :, :, :, hi].reshape(256, CHIP), wd[n : n + wide, :])
             part[s, :, :, GU + n : GU + n + wide] = got.astype(BF).reshape(4, 64, wide)
 
-    def add_relay(k):
-        s = k % 2
-
-        @pl.loop(0, 7)
-        def _(n):
-            cols = pl.ds(pl.multiple_of(n * 384, 128), 384)
+    def add_relay(k, a):
+        s = k % 2
+        base, count = (GU, 7) if a == 1 else (0, 14)
+
+        @pl.loop(0, count)
+        def _(n):
+            cols = pl.ds(pl.multiple_of(base + n * 128, 128), 128)
             part[s, up, 0:32, cols] = (part[s, up, 0:32, cols].astype(F32) + rel[k, 0, :, cols].astype(F32)).astype(BF)
             part[s, dn, 32:64, cols] = (part[s, dn, 32:64, cols].astype(F32) + rel[k, 1, :, cols].astype(F32)).astype(BF)
 
@@ -251,7 +265,16 @@
             hid[k, y, :, pl.ds(pl.multiple_of(FF + n * 128, 128), 128)] = d_gate.astype(BF)
             hid[k, y, :, pl.ds(pl.multiple_of(GU + n * 128, 128), 128)] = (back * activ).astype(BF)
 
-    def products(k):
+    def products_back(k):
+        s = k % 2
+
+        @pl.loop(0, 4)
+        def _(n):
+            cols = pl.ds(pl.multiple_of(n * 256, 256), 256)
+            got = mm_nt(hid[k, :, :, FF:ALL].reshape(256, GU), wgu[cols, :])
+            outp[s, :, :, :, pl.ds(pl.multiple_of(CHIP + n * 256, 256), 256)] = got.astype(BF).reshape(4, 4, TOK, 256)
+
+    def products_out(k):
         s = k % 2
 
         @pl.loop(0, 4)
@@ -259,8 +282,6 @@
             cols = pl.ds(pl.multiple_of(n * 256, 256), 256)
             got = mm(hid[k, :, :, 0:FF].reshape(256, FF), wd[:, cols])
             outp[s, :, :, :, cols] = got.astype(BF).reshape(4, 4, TOK, 256)
-            got = mm_nt(hid[k, :, :, FF:ALL].reshape(256, GU), wgu[cols, :])
-            outp[s, :, :, :, pl.ds(pl.multiple_of(CHIP + n * 256, 256), 256)] = got.astype(BF).reshape(4, 4, TOK, 256)
 
     def weight_sums(k):
         xt[...] = gath[k, :, :, :, lo].reshape(256, CHIP).T
@@ -282,28 +303,23 @@
             for m, high in ((0, 256), (256, 256), (512, 256), (768, 128)):
                 acc_d[m : m + high, cols] += mm(ht[m : m + high, :], cots)
 
-    def sum_first(k):
+    def sum_first(k, a):
         s = k % 2
         for i in range(4):
-            total = outp[s, i, x, :, lo].astype(F32)
+            for h in range(2):
+                total = (outp[s, i, x, :, strip(a, 0)] if h == 0 else outp[s, z, i, :, strip(a, 1)]).astype(F32)
+                for j in range(3):
+                    total += rs1[k, a, h, j, i].astype(F32)
+                sum1[k, a, h, i] = total.astype(BF)
+
+    def sum_last(k, a):
+        to = bw if a == 1 else fw
+        rows = pl.ds(pl.multiple_of(k * TOK, TOK), TOK)
+        for h in range(2):
+            total = sum1[k, a, h, z if h == 0 else x].astype(F32)
             for j in range(3):
-                total += rs1[k, 0, j, i].astype(F32)
-            sum1[k, 0, i] = total.astype(BF)
-            total = outp[s, z, i, :, hi].astype(F32)
-            for j in range(3):
-                total += rs1[k, 1, j, i].astype(F32)
-            sum1[k, 1, i] = total.astype(BF)
-
-    def sum_last(k):
-        rows = pl.ds(pl.multiple_of(k * TOK, TOK), TOK)
-        total = sum1[k, 0, z].astype(F32)
-        for j in range(3):
-            total += rs2[k, 0, j].astype(F32)
-        fw[rows, :] = total
-        total = sum1[k, 1, x].astype(F32)
-        for j in range(3):
-            total += rs2[k, 1, j].astype(F32)
-        bw[rows, :] = total
+                total += rs2[k, a, h, j].astype(F32)
+            to[rows, h * WIDE : (h + 1) * WIDE] = total
 
     exchange = [
         rc(send_gu, recv_gu, w_s.at[0], w_r.at[0], twin),
@@ -317,45 +333,55 @@
         @pl.when(at(i - 2))
         def _():
             k = i - 2
-            finish(quarter(k, k % 2))
+            finish(quarter(k, k % 2, 1))
+            finish(quarter(k, k % 2, 0))
             activate(k)
-            start(share(k))
+            start(share(k, 0))
+            start(share(k, 1))
 
         @pl.when(at(i - 1))
         def _():
             k = i - 1
-            finish(relay(k, k % 2))
-            add_relay(k)
-            start(quarter(k, k % 2))
+            for a in (1, 0):
+                finish(relay(k, k % 2, a))
+                add_relay(k, a)
+                start(quarter(k, k % 2, a))
+
+        @pl.when(i < CHUNKS)
+        def _():
+            finish(rest(i, 1))
+            project_back(i)
+            start(relay(i, i % 2, 1))
+            finish(rest(i, 0))
+            project_pre(i)
+            start(relay(i, i % 2, 0))
 
         @pl.when(i + 1 < CHUNKS)
         def _():
-            finish(gather_x(i + 1) + gather_z(i + 1))
-            start(gather_rest(i + 1))
+            for a in (1, 0):
+                finish(near(i + 1, a))
+                start(rest(i + 1, a))
 
         @pl.when(i + 2 < CHUNKS)
         def _():
-            start(gather_x(i + 2) + gather_z(i + 2))
-
-        @pl.when(i < CHUNKS)
-        def _():
-            finish(gather_rest(i))
-            project(i)
-            start(relay(i, i % 2))
+            start(near(i + 2, 1) + near(i + 2, 0))
 
         @pl.when(at(i - 4))
         def _():
             k = i - 4
-            finish(scatter(k, k % 2))
-            sum_first(k)
-            start(scatter_rest(k))
+            for a in (1, 0):
+                finish(scatter(k, k % 2, a))
+                sum_first(k, a)
+                start(scatter_rest(k, a))
 
         @pl.when(at(i - 3))
         def _():
             k = i - 3
-            finish(pass_on(k))
-            products(k)
-            start(scatter(k, k % 2))
+            finish(share(k, 1) + pass_on(k))
+            products_back(k)
+            start(scatter(k, k % 2, 1))
+            products_out(k)
+            start(scatter(k, k % 2, 0))
             weight_sums(k)
 
         @pl.when(i - 3 == CHUNKS - 1)
@@ -371,37 +397,42 @@
 
         @pl.when(at(i - 5))
         def _():
-            k = i - 5
-            finish(scatter_rest(k))
-            sum_last(k)
+            for a in (1, 0):
+                finish(scatter_rest(i - 5, a))
+                sum_last(i - 5, a)
 
         @pl.when(at(i - 2))
         def _():
-            k = i - 2
-            finish(share(k))
-            start(pass_on(k))
+            finish(share(i - 2, 0))
+            start(pass_on(i - 2))
 
         return carry
 
-    lax.fori_loop(0, CHUNKS + 5, step, 0)
-
+    lax.fori_loop(0, CHUNKS + 4, step, 0)
+
+    finish(scatter_rest(CHUNKS - 1, 1))
+    sum_last(CHUNKS - 1, 1)
+    inv = invb[:, 0:1]
     pull = jnp.sum(tokb[...].astype(F32) * gainb[0:1, :] * bw[...], axis=1, keepdims=True)
-    rmsb[y] = jnp.broadcast_to(pull, (HALF, 128)) * invb[...]
+    rmsb[y] = to_lanes(pull * inv)
     sends = [rc(rmsb.at[y], rmsb.at[y], m_s.at[j - 1], m_r.at[j - 1], ydev(j)) for j in (1, 2, 3)]
     start(sends)
+    finish(scatter_rest(CHUNKS - 1, 0))
+    sum_last(CHUNKS - 1, 0)
     mixb[...] = (tokb[...].astype(F32) + fw[...]).astype(BF)
+    back = [
+        rc(mixb.at[:, theirs], mixed_ref.at[my_rows, :], o_s.at[0], o_r.at[0], twin),
+        rc(igb.at[:, theirs], ig_ref.at[my_rows, :], o_s.at[1], o_r.at[1], twin),
+    ]
+    start(back[0:1])
     mixed_ref[my_rows, :] = mixb[:, mine]
-    back = [rc(mixb.at[:, theirs], mixed_ref.at[my_rows, :], o_s.at[0], o_r.at[0], twin)]
-    start(back)
     finish(sends)
-    inv = invb[:, 0:1]
-    fix = inv * inv * ((rmsb[0] + rmsb[1]) + (rmsb[2] + rmsb[3]))[:, 0:1] / MODEL
+    fix = inv * inv * to_column(((rmsb[0] + rmsb[1]) + (rmsb[2] + rmsb[3]))[0:1, :]) / MODEL
     igb[...] = (
         cotb[...].astype(F32) + gainb[0:1, :] * (inv * bw[...]) - tokb[...].astype(F32) * fix
     ).astype(BF)
+    start(back[1:2])
     ig_ref[my_rows, :] = igb[:, mine]
-    back += [rc(igb.at[:, theirs], ig_ref.at[my_rows, :], o_s.at[1], o_r.at[1], twin)]
-    start(back[1:])
 
     finish(exchange)
 
@@ -424,9 +455,17 @@
             cols = slice(j * 128, j * 128 + 128)
             src = pl.ds(pl.multiple_of(c * WIDE + j * 128, 128), 128)
             total = acc_d[rows, src] + recv_d[rows, cols].astype(F32)
-            dg_ref[rows, cols] = (total * dm_ref[i, j].astype(F32)).astype(BF)
+            dg_ref[rows, cols] = (total * dm_ref[j, i].astype(F32)).astype(BF)
 
     finish(back)
+
+
+def store(*refs):
+    copies = [pltpu.make_async_copy(refs[i], refs[5 + i], refs[10].at[i]) for i in range(5)]
+    for copy in copies:
+        copy.start()
+    for copy in copies:
+        copy.wait()
 
 
 def shards(tokens, cotangent, norm_gain, gate_w, up_w, down_w, gate_b, up_b, down_b):
@@ -437,15 +476,14 @@
         return [pltpu.SemaphoreType.DMA(shape)] * 2
 
     V = pltpu.VMEM
-    out = jax.ShapeDtypeStruct
-    return pl.pallas_call(
+    results = pl.pallas_call(
         body,
         out_shape=(
-            out(tokens.shape, BF),
-            out(tokens.shape, BF),
-            out(gate_w.shape, BF),
-            out(up_w.shape, BF),
-            out(down_w.shape, BF),
+            V(tokens.shape, BF),
+            V(tokens.shape, BF),
+            V(gate_w.shape, BF),
+            V(up_w.shape, BF),
+            V(down_w.shape, BF),
         ),
         in_specs=[vmem] * 6 + [smem] * 3,
         out_specs=(vmem,) * 5,
@@ -454,9 +492,9 @@
             V((HALF, CHIP), BF),
             V((8, WIDE), F32),
             V((8, CHIP), F32),
-            V((4, HALF, 128), F32),
+            V((4, 8, 128), F32),
             V((HALF, 128), F32),
-            V((4, HALF, 128), F32),
+            V((4, 8, 128), F32),
             V((CHUNKS, 4, 4, TOK, 2 * CHIP), BF),
             V((CHIP, GU), BF),
             V((FF, CHIP), BF),
@@ -465,9 +503,9 @@
             V((CHUNKS, 2, 64, ALL), BF),
             V((CHUNKS, 4, 64, ALL), BF),
             V((2, 4, 4, TOK, 2 * CHIP), BF),
-            V((CHUNKS, 2, 3, 4, TOK, CHIP), BF),
-            V((CHUNKS, 2, 4, TOK, CHIP), BF),
-            V((CHUNKS, 2, 3, TOK, CHIP), BF),
+            V((CHUNKS, 2, 2, 3, 4, TOK, WIDE), BF),
+            V((CHUNKS, 2, 2, 4, TOK, WIDE), BF),
+            V((CHUNKS, 2, 2, 3, TOK, WIDE), BF),
             V((HALF, CHIP), F32),
             V((HALF, CHIP), F32),
             V((CHIP, GU), F32),
@@ -483,23 +521,31 @@
         ]
         + dma(5)
         + dma(3)
-        + dma(CHUNKS, 2, 3)
-        + dma(CHUNKS, 2, 3)
+        + dma(CHUNKS, 2, 2, 3)
+        + dma(CHUNKS, 2, 2, 3)
+        + dma(CHUNKS, 2, 2)
+        + dma(CHUNKS, 2, 2)
+        + dma(CHUNKS, 2, 2)
         + dma(CHUNKS, 2)
-        + dma(CHUNKS, 2)
-        + dma(CHUNKS, 2)
-        + dma(CHUNKS, 2)
-        + dma(CHUNKS, 2, 3)
-        + dma(CHUNKS, 2, 3)
+        + dma(CHUNKS, 2, 2, 3)
+        + dma(CHUNKS, 2, 2, 3)
         + dma(2)
         + dma(3)
         + dma(2),
         compiler_params=pltpu.CompilerParams(
-            collective_id=0, has_side_effects=True, vmem_limit_bytes=62 * 1024 * 1024
+            collective_id=0, has_side_effects=True, vmem_limit_bytes=54 * 1024 * 1024
         ),
         cost_estimate=pl.CostEstimate(flops=17_000_000_000, bytes_accessed=6_000_000, transcendentals=2_000_000),
         name="ffn",
-    )(tokens, cotangent, norm_gain.reshape(1, -1), gate_w, up_w, down_w, gate_b, up_b, down_b)
+    )(tokens, cotangent, norm_gain.reshape(1, -1), gate_w, up_w, down_w, gate_b, up_b, down_b.T)
+    return pl.pallas_call(
+        store,
+        out_shape=tuple(jax.ShapeDtypeStruct(r.shape, r.dtype) for r in results),
+        in_specs=[vmem] * 5,
+        out_specs=(pl.BlockSpec(memory_space=pl.ANY),) * 5,
+        scratch_shapes=[pltpu.SemaphoreType.DMA((5,))],
+        name="store",
+    )(*[pltpu.with_memory_space_constraint(r, pltpu.VMEM) for r in results])
 
 
 def solution(mesh):

time: 156 us -> 142 us (0.910)
  local copies, waits for them, and re-layouts: 8.31 us -> 0 us
  Pallas kernels: 147 us -> 142 us
    unnamed x12 -> x0, local copies, waits for them, and re-layouts: 8.31 us -> none
    pallas_call x1 -> x2, Pallas kernels: 147 us -> 142 us  [the longest x1 140 us: shards(): pl.pallas_call(body, out_shape=(V(tokens.shape, BF), V(tokens.shape, BF),...]
where the time goes in v2:
time: 142 us
  Pallas kernels  142 us (100%)
    pallas_call x1, Pallas kernels, shards(): pl.pallas_call(body, out_shape=(V(tokens.shape, BF), V(tokens.shape, BF),...  140 us

profile of v2, /device:TPU:1, one launch (start us, length us, event | category | flops | bytes accessed | tf_op | source)
XLA Modules:
  0.0 142.3 jit_solution(3899222735590697430)
XLA Ops:
  0.6 140.0 %ffn.1 = (bf16[128,512]{1,0:T(8,128)(2,1)S(1)}, bf16[128,512]{1,0:T(8,128)(2,1)S(1)}, bf16[512,896]{1,0:T(8,128)(2,1)S(1)}, bf16[512,896]{1,0:T(8,128)(2,1)S(1)}, bf16[896,512]{1,0:T(8,128)(2,1)S(1)}) custom-call(bf16[128,512]{1,0:T(8,128)(2,1)} %tok_ref.1, bf16[128,512]{1,0:T(8,128)(2,1)} %cot_ref.1, f32[1,512]{1,0:T(1,128)} %bitcast.2, ...), custom_call_target="tpu_custom_call" | custom-call | flops 16999999488 | bytes 6000000 | tf_op jit(solution)/shard_map/ffn/pallas_call | solution.py:479
  140.7 1.7 %store.1 = (bf16[128,512]{1,0:T(8,128)(2,1)}, bf16[128,512]{1,0:T(8,128)(2,1)}, bf16[512,896]{1,0:T(8,128)(2,1)}, bf16[512,896]{1,0:T(8,128)(2,1)}, bf16[896,512]{1,0:T(8,128)(2,1)}) custom-call(bf16[128,512]{1,0:T(8,128)(2,1)S(1)} %get-tuple-element.10.refs_0_, bf16[128,512]{1,0:T(8,128)(2,1)S(1)} %get-tuple-element.11.refs_1_, ...), custom_call_target="tpu_custom_call" | custom-call | tf_op jit(solution)/shard_map/store/pallas_call | solution.py:541

commit v3 on v2

--- a/solution.py
+++ b/solution.py
@@ -32,10 +32,11 @@
 def body(
     tok_ref, cot_ref, gain_ref, gw_ref, uw_ref, dw_ref, gm_ref, um_ref, dm_ref,
     mixed_ref, ig_ref, gg_ref, ug_ref, dg_ref,
-    tokb, cotb, gain8, gainb, ssq, invb, rmsb, gath, wgu, wd, part, rel, full, hid, outp, rs1, sum1, rs2,
-    fw, bw, acc_gu, acc_d, xt, ht, send_gu, send_d, recv_gu, recv_d, mixb, igb,
-    sw_s, sw_r, sq_s, sq_r, p1_s, p1_r, p2_s, p2_r, r_s, r_r, f_s, f_r, g_s, g_r, h_s, h_r,
-    a_s, a_r, b_s, b_r, w_s, w_r, m_s, m_r, o_s, o_r,
+    gwb, uwb, dwb, tokn, cotn, tokb, cotb, gain8, gainb, ssq, invb, invn, pulls, totals,
+    gath, wgu, wd, part, rel, full, hid, outp, rs1, sum1, rs2,
+    acc_gu, acc_d, xt, ht, send_gu, send_d, recv_gu, recv_d,
+    l_s, sw_s, sw_r, sq_s, sq_r, p1_s, p1_r, p2_s, p2_r, r_s, r_r, f_s, f_r, t_s, t_r, g_s, g_r, h_s, h_r,
+    a_s, a_r, b_s, b_r, w_s, w_r,
 ):
     row = lax.axis_index("row")
     col = lax.axis_index("col")
@@ -91,10 +92,77 @@
     my_rows = pl.ds(pl.multiple_of(c * HALF, HALF), HALF)
     their_rows = pl.ds(pl.multiple_of(other * HALF, HALF), HALF)
 
+    def width(a):
+        return WIDE + 128 * (1 - a)
+
+    def out_strip(a, h):
+        return pl.ds(2 * (WIDE + 128) * a + h * width(a), width(a))
+
     barrier = pltpu.get_barrier_semaphore()
     peers = [twin] + [f(j) for f in (xdev, ydev, zdev) for j in (1, 2, 3)]
+    peers += [dev((z + j) % 4, x, y, other) for j in (1, 2, 3)] + [dev(z, (x + j) % 4, y, other) for j in (1, 2, 3)]
     for peer in peers:
         pl.semaphore_signal(barrier, inc=1, device_id=peer, device_id_type=MESH)
+
+    loads = [
+        pltpu.make_async_copy(src, dst, l_s.at[n])
+        for n, (src, dst) in enumerate(
+            ((cot_ref, cotn), (tok_ref, tokn), (dw_ref, dwb), (gw_ref, gwb), (uw_ref, uwb))
+        )
+    ]
+    start(loads)
+    gain8[...] = jnp.broadcast_to(gain_ref[...], (8, WIDE))
+    gainb[:, mine] = gain8[...]
+    finish(loads[0:2])
+    tokb[:, mine] = tokn[my_rows, :]
+    cotb[:, mine] = cotn[my_rows, :]
+    finish(loads[2:3])
+
+    @pl.loop(0, 7)
+    def _(i):
+        rows = pl.ds(pl.multiple_of(i * 128, 128), 128)
+        for j in range(4):
+            to = pl.ds(pl.multiple_of(c * WIDE + j * 128, 128), 128)
+            keep = dm_ref[j, i].astype(F32)
+            wd[rows, to] = (dwb[rows, j * 128 : j * 128 + 128].astype(F32) * keep).astype(BF)
+
+    pl.semaphore_wait(barrier, len(peers))
+
+    swaps = [
+        rc(cotn.at[their_rows, :], cotb.at[:, mine], sw_s.at[0], sw_r.at[0], twin),
+        rc(tokn.at[their_rows, :], tokb.at[:, mine], sw_s.at[1], sw_r.at[1], twin),
+        rc(gain8, gainb.at[:, mine], sw_s.at[2], sw_r.at[2], twin),
+        rc(wd.at[:, mine], wd.at[:, mine], sw_s.at[3], sw_r.at[3], twin),
+        rc(wgu.at[mine, :], wgu.at[mine, :], sw_s.at[4], sw_r.at[4], twin),
+        rc(invn.at[my_rows, :], invn.at[my_rows, :], sw_s.at[5], sw_r.at[5], twin),
+    ]
+    start(swaps[0:4])
+
+    def near(k, a):
+        def one(h, to, j):
+            block = gath.at[k, z, x, :, strip(a, h)]
+            return rc(block, block, p1_s.at[k, a, h, j - 1], p1_r.at[k, a, h, j - 1], to(j))
+
+        return [one(h, to, j) for j in (1, 2, 3) for h, to in ((0, xdev), (1, zdev))]
+
+    def rest(k, a):
+        def one(h, to, j):
+            block = gath.at[k, z, :, :, strip(a, 0)] if h == 0 else gath.at[k, :, x, :, strip(a, 1)]
+            return rc(block, block, p2_s.at[k, a, h, j - 1], p2_r.at[k, a, h, j - 1], to(j))
+
+        return [one(h, to, j) for j in (1, 2, 3) for h, to in ((0, zdev), (1, xdev))]
+
+    finish(swaps[0:1])
+    for k in range(CHUNKS):
+        gath[k, z, x, :, hi] = cotb[k * TOK : (k + 1) * TOK, :]
+    start(near(0, 1))
+
+    finish(swaps[1:3])
+    tok = tokb[...].astype(F32)
+    ssq[y] = to_lanes(jnp.sum(tok * tok, axis=1, keepdims=True))
+    sends = [rc(ssq.at[y], ssq.at[y], sq_s.at[j - 1], sq_r.at[j - 1], ydev(j)) for j in (1, 2, 3)]
+    start(sends)
+    finish(loads[3:5])
 
     @pl.loop(0, 4)
     def _(i):
@@ -103,58 +171,11 @@
         for j in range(7):
             cols = slice(j * 128, j * 128 + 128)
             keep = gm_ref[i, j].astype(F32)
-            wgu[to, j * 128 : j * 128 + 128] = (gw_ref[rows, cols].astype(F32) * keep).astype(BF)
+            wgu[to, j * 128 : j * 128 + 128] = (gwb[rows, cols].astype(F32) * keep).astype(BF)
             keep = um_ref[i, j].astype(F32)
-            wgu[to, FF + j * 128 : FF + j * 128 + 128] = (uw_ref[rows, cols].astype(F32) * keep).astype(BF)
-
-    @pl.loop(0, 7)
-    def _(i):
-        rows = pl.ds(pl.multiple_of(i * 128, 128), 128)
-        for j in range(4):
-            to = pl.ds(pl.multiple_of(c * WIDE + j * 128, 128), 128)
-            keep = dm_ref[j, i].astype(F32)
-            wd[rows, to] = (dw_ref[rows, j * 128 : j * 128 + 128].astype(F32) * keep).astype(BF)
-
-    gain8[...] = jnp.broadcast_to(gain_ref[...], (8, WIDE))
-    tokb[:, mine] = tok_ref[my_rows, :]
-    cotb[:, mine] = cot_ref[my_rows, :]
-    gainb[:, mine] = gain8[...]
-
-    pl.semaphore_wait(barrier, len(peers))
-
-    swaps = [
-        rc(cot_ref.at[their_rows, :], cotb.at[:, mine], sw_s.at[0], sw_r.at[0], twin),
-        rc(tok_ref.at[their_rows, :], tokb.at[:, mine], sw_s.at[1], sw_r.at[1], twin),
-        rc(gain8, gainb.at[:, mine], sw_s.at[2], sw_r.at[2], twin),
-        rc(wd.at[:, mine], wd.at[:, mine], sw_s.at[3], sw_r.at[3], twin),
-        rc(wgu.at[mine, :], wgu.at[mine, :], sw_s.at[4], sw_r.at[4], twin),
-    ]
-    start(swaps)
-
-    def near(k, a):
-        def one(h, to, j):
-            block = gath.at[k, z, x, :, strip(a, h)]
-            return rc(block, block, p1_s.at[k, a, h, j - 1], p1_r.at[k, a, h, j - 1], to(j))
-
-        return [one(h, to, j) for j in (1, 2, 3) for h, to in ((0, xdev), (1, zdev))]
-
-    def rest(k, a):
-        def one(h, to, j):
-            block = gath.at[k, z, :, :, strip(a, 0)] if h == 0 else gath.at[k, :, x, :, strip(a, 1)]
-            return rc(block, block, p2_s.at[k, a, h, j - 1], p2_r.at[k, a, h, j - 1], to(j))
-
-        return [one(h, to, j) for j in (1, 2, 3) for h, to in ((0, zdev), (1, xdev))]
-
-    finish(swaps[0:1])
-    for k in range(CHUNKS):
-        gath[k, z, x, :, hi] = cotb[k * TOK : (k + 1) * TOK, :]
-    start(near(0, 1))
-
-    finish(swaps[1:3])
-    tok = tokb[...].astype(F32)
-    ssq[y] = to_lanes(jnp.sum(tok * tok, axis=1, keepdims=True))
-    sends = [rc(ssq.at[y], ssq.at[y], sq_s.at[j - 1], sq_r.at[j - 1], ydev(j)) for j in (1, 2, 3)]
-    start(sends)
+            wgu[to, FF + j * 128 : FF + j * 128 + 128] = (uwb[rows, cols].astype(F32) * keep).astype(BF)
+
+    start(swaps[4:5])
     finish(near(0, 1))
     start(rest(0, 1))
     finish(sends)
@@ -165,6 +186,8 @@
         scaled = tokb[rows, :].astype(F32) * gainb[0:1, :] * invb[rows, 0:1]
         gath[k, z, x, :, lo] = scaled.astype(BF)
     start(near(0, 0))
+    invn[my_rows, :] = invb[...]
+    start(swaps[5:6])
 
     @pl.loop(0, 16)
     def _(i):
@@ -174,7 +197,7 @@
     finish(near(0, 0))
     start(rest(0, 0))
     start(near(1, 1) + near(1, 0))
-    finish(swaps[3:5])
+    finish(swaps[3:6])
 
     def span(a):
         return pl.ds(GU, FF) if a == 1 else pl.ds(0, GU)
@@ -193,35 +216,68 @@
             rc(part.at[s, dn, :, span(a)], full.at[k, 1, :, span(a)], f_s.at[k, a, 1], f_r.at[k, a, 1], dn_dev),
         ]
 
-    def share(k, later):
-        one = hid.at[k, y, pl.ds(32 if later else 0, 32), :]
-        two = hid.at[k, y, pl.ds(0 if later else 32, 32), :]
+    def kind(b):
+        return pl.ds(FF, GU) if b == 1 else pl.ds(0, FF)
+
+    def share(k, b, later):
+        one = hid.at[k, y, pl.ds(32 if later else 0, 32), kind(b)]
+        two = hid.at[k, y, pl.ds(0 if later else 32, 32), kind(b)]
         return [
-            rc(one, one, g_s.at[k, later, 0], g_r.at[k, later, 0], up_dev),
-            rc(two, two, g_s.at[k, later, 1], g_r.at[k, later, 1], dn_dev),
+            rc(one, one, g_s.at[k, b, later, 0], g_r.at[k, b, later, 0], up_dev),
+            rc(two, two, g_s.at[k, b, later, 1], g_r.at[k, b, later, 1], dn_dev),
         ]
 
-    def pass_on(k):
-        first = hid.at[k, dn, pl.ds(0, 32), :]
-        second = hid.at[k, up, pl.ds(32, 32), :]
+    def pass_on(k, b):
+        first = hid.at[k, dn, pl.ds(0, 32), kind(b)]
+        second = hid.at[k, up, pl.ds(32, 32), kind(b)]
         return [
-            rc(first, first, h_s.at[k, 0], h_r.at[k, 0], up_dev),
-            rc(second, second, h_s.at[k, 1], h_r.at[k, 1], dn_dev),
+            rc(first, first, h_s.at[k, b, 0], h_r.at[k, b, 0], up_dev),
+            rc(second, second, h_s.at[k, b, 1], h_r.at[k, b, 1], dn_dev),
         ]
+
+    def tell(k):
+        return [rc(pulls.at[k, y], pulls.at[k, y], t_s.at[k, j - 1], t_r.at[k, j - 1], ydev(j)) for j in (1, 2, 3)]
 
     def scatter(k, s, a):
         def one(h, to, j):
-            block = outp.at[s, :, (x + j) % 4, :, strip(a, 0)] if h == 0 else outp.at[s, (z + j) % 4, :, :, strip(a, 1)]
-            return rc(block, rs1.at[k, a, h, j - 1], a_s.at[k, a, h, j - 1], a_r.at[k, a, h, j - 1], to(j))
+            strip_a = out_strip(a, h)
+            block = outp.at[s, :, (x + j) % 4, :, strip_a] if h == 0 else outp.at[s, (z + j) % 4, :, :, strip_a]
+            return rc(
+                block, rs1.at[k, a, h, j - 1, :, :, pl.ds(0, width(a))],
+                a_s.at[k, a, h, j - 1], a_r.at[k, a, h, j - 1], to(j),
+            )
 
         return [one(h, to, j) for j in (1, 2, 3) for h, to in ((0, xdev), (1, zdev))]
 
+    at_mine = z * other + x * c
+    at_theirs = z * c + x * other
+
     def scatter_rest(k, a):
-        def one(h, to, j):
-            block = sum1.at[k, a, h, ((z if h == 0 else x) + j) % 4]
-            return rc(block, rs2.at[k, a, h, j - 1], b_s.at[k, a, h, j - 1], b_r.at[k, a, h, j - 1], to(j))
-
-        return [one(h, to, j) for j in (1, 2, 3) for h, to in ((0, zdev), (1, xdev))]
+        def one(h, place, send, j, to):
+            return rc(
+                sum1.at[k, a, h, place, :, pl.ds(0, width(a))], rs2.at[k, a, c, j, :, pl.ds(0, width(a))],
+                send, b_r.at[k, a, c, j], to,
+            )
+
+        far = [
+            one(h, ((x if h else z) + j) % 4, b_s.at[k, a, h, j], j,
+                dev(z, (x + j) % 4, y, 1) if h else dev((z + j) % 4, x, y, 0))
+            for j in (1, 2, 3) for h in (0, 1)
+        ]
+        return far + [one(other, at_theirs, b_s.at[k, a, 0, 0], 0, twin)]
+
+    def await_rest(k, a):
+        for copy in scatter_rest(k, a):
+            copy.wait_send()
+
+        def arrival(core, j):
+            place = rs2.at[k, a, core, j, :, pl.ds(0, width(a))]
+            rc(place, place, b_s.at[k, a, 0, 0], b_r.at[k, a, core, j], twin).wait_recv()
+
+        arrival(other, 0)
+        for j in (1, 2, 3):
+            arrival(0, j)
+            arrival(1, j)
 
     def project_pre(k):
         s = k % 2
@@ -251,8 +307,7 @@
     def activate(k):
         s = k % 2
 
-        @pl.loop(0, 7)
-        def _(n):
+        def one(n, pulled):
             def total(base):
                 cols = pl.ds(pl.multiple_of(base + n * 128, 128), 128)
                 return part[s, y, :, cols].astype(F32) + full[k, 0, :, cols].astype(F32) + full[k, 1, :, cols].astype(F32)
@@ -261,9 +316,14 @@
             sigma = jax.nn.sigmoid(gate)
             activ = gate * sigma
             d_gate = back * up_value * sigma * (1.0 + gate * (1.0 - sigma))
+            d_up = back * activ
             hid[k, y, :, pl.ds(pl.multiple_of(n * 128, 128), 128)] = (activ * up_value).astype(BF)
             hid[k, y, :, pl.ds(pl.multiple_of(FF + n * 128, 128), 128)] = d_gate.astype(BF)
-            hid[k, y, :, pl.ds(pl.multiple_of(GU + n * 128, 128), 128)] = (back * activ).astype(BF)
+            hid[k, y, :, pl.ds(pl.multiple_of(GU + n * 128, 128), 128)] = d_up.astype(BF)
+            return pulled + (d_gate * gate + d_up * up_value)
+
+        pulled = lax.fori_loop(0, 7, one, jnp.zeros((HALF, 128), F32))
+        pulls[k, y] = to_lanes(jnp.sum(pulled, axis=1, keepdims=True))
 
     def products_back(k):
         s = k % 2
@@ -272,7 +332,7 @@
         def _(n):
             cols = pl.ds(pl.multiple_of(n * 256, 256), 256)
             got = mm_nt(hid[k, :, :, FF:ALL].reshape(256, GU), wgu[cols, :])
-            outp[s, :, :, :, pl.ds(pl.multiple_of(CHIP + n * 256, 256), 256)] = got.astype(BF).reshape(4, 4, TOK, 256)
+            outp[s, :, :, :, pl.ds(pl.multiple_of(2 * (WIDE + 128) + n * 256, 256), 256)] = got.astype(BF).reshape(4, 4, TOK, 256)
 
     def products_out(k):
         s = k % 2
@@ -281,11 +341,16 @@
         def _(n):
             cols = pl.ds(pl.multiple_of(n * 256, 256), 256)
             got = mm(hid[k, :, :, 0:FF].reshape(256, FF), wd[:, cols])
-            outp[s, :, :, :, cols] = got.astype(BF).reshape(4, 4, TOK, 256)
-
-    def weight_sums(k):
+            to = pl.ds(pl.multiple_of(n * 256 + (n // 2) * 128, 128), 256)
+            outp[s, :, :, :, to] = got.astype(BF).reshape(4, 4, TOK, 256)
+
+        for i in range(4):
+            pulled = jnp.broadcast_to(to_column(pulls[k, i, 0:1, :]), (HALF, 128)).astype(BF).reshape(4, TOK, 128)
+            outp[s, i, :, :, WIDE : WIDE + 128] = pulled
+            outp[s, i, :, :, 2 * WIDE + 128 : 2 * WIDE + 256] = pulled
+
+    def sums_gu(k):
         xt[...] = gath[k, :, :, :, lo].reshape(256, CHIP).T
-        ht[...] = hid[k, :, :, 0:FF].reshape(256, FF).T
 
         @pl.loop(0, 7)
         def _(n):
@@ -295,6 +360,9 @@
             for m in range(4):
                 acc_gu[m * 256 : m * 256 + 256, cols] += mm(xt[m * 256 : m * 256 + 256, :], pulled)
 
+    def sums_d(k):
+        ht[...] = hid[k, :, :, 0:FF].reshape(256, FF).T
+
         @pl.loop(0, 4)
         def _(n):
             cols = pl.ds(pl.multiple_of(n * 256, 256), 256)
@@ -307,19 +375,26 @@
         s = k % 2
         for i in range(4):
             for h in range(2):
-                total = (outp[s, i, x, :, strip(a, 0)] if h == 0 else outp[s, z, i, :, strip(a, 1)]).astype(F32)
+                total = (outp[s, i, x, :, out_strip(a, 0)] if h == 0 else outp[s, z, i, :, out_strip(a, 1)]).astype(F32)
                 for j in range(3):
-                    total += rs1[k, a, h, j, i].astype(F32)
-                sum1[k, a, h, i] = total.astype(BF)
+                    total += rs1[k, a, h, j, i, :, 0 : width(a)].astype(F32)
+                sum1[k, a, h, i, :, 0 : width(a)] = total.astype(BF)
 
     def sum_last(k, a):
-        to = bw if a == 1 else fw
-        rows = pl.ds(pl.multiple_of(k * TOK, TOK), TOK)
-        for h in range(2):
-            total = sum1[k, a, h, z if h == 0 else x].astype(F32)
-            for j in range(3):
-                total += rs2[k, a, h, j].astype(F32)
-            to[rows, h * WIDE : (h + 1) * WIDE] = total
+        for core, first in ((c, sum1[k, a, c, at_mine, :, 0 : width(a)]), (other, rs2[k, a, other, 0, :, 0 : width(a)])):
+            rows = pl.ds(pl.multiple_of(core * HALF + k * TOK, TOK), TOK)
+            total = first.astype(F32)
+            for j in (1, 2, 3):
+                total += rs2[k, a, core, j, :, 0 : width(a)].astype(F32)
+            if a == 0:
+                mixed_ref[rows, :] = (tokn[rows, :].astype(F32) + total[:, 0:WIDE]).astype(BF)
+                totals[rows, :] = total[:, WIDE:]
+            else:
+                inv = invn[rows, 0:1]
+                fix = inv * inv * totals[rows, 0:1] / MODEL
+                ig_ref[rows, :] = (
+                    cotn[rows, :].astype(F32) + gain8[0:1, :] * (inv * total) - tokn[rows, :].astype(F32) * fix
+                ).astype(BF)
 
     exchange = [
         rc(send_gu, recv_gu, w_s.at[0], w_r.at[0], twin),
@@ -336,8 +411,9 @@
             finish(quarter(k, k % 2, 1))
             finish(quarter(k, k % 2, 0))
             activate(k)
-            start(share(k, 0))
-            start(share(k, 1))
+            start(tell(k))
+            for b in (0, 1):
+                start(share(k, b, 0) + share(k, b, 1))
 
         @pl.when(at(i - 1))
         def _():
@@ -369,7 +445,7 @@
         @pl.when(at(i - 4))
         def _():
             k = i - 4
-            for a in (1, 0):
+            for a in (0, 1):
                 finish(scatter(k, k % 2, a))
                 sum_first(k, a)
                 start(scatter_rest(k, a))
@@ -377,12 +453,23 @@
         @pl.when(at(i - 3))
         def _():
             k = i - 3
-            finish(share(k, 1) + pass_on(k))
+            finish(tell(k) + share(k, 0, 1) + pass_on(k, 0))
+            products_out(k)
+            start(scatter(k, k % 2, 0))
+            sums_d(k)
+
+        @pl.when(i - 3 == CHUNKS - 1)
+        def _():
+            send_d[...] = acc_d[:, theirs].astype(BF)
+            start(exchange[1:])
+
+        @pl.when(at(i - 3))
+        def _():
+            k = i - 3
+            finish(share(k, 1, 1) + pass_on(k, 1))
             products_back(k)
             start(scatter(k, k % 2, 1))
-            products_out(k)
-            start(scatter(k, k % 2, 0))
-            weight_sums(k)
+            sums_gu(k)
 
         @pl.when(i - 3 == CHUNKS - 1)
         def _():
@@ -392,48 +479,26 @@
                 src = pl.ds(pl.multiple_of(other * WIDE + n * 128, 128), 128)
                 send_gu[rows, :] = acc_gu[src, :].astype(BF)
 
-            send_d[...] = acc_d[:, theirs].astype(BF)
-            start(exchange)
+            start(exchange[0:1])
 
         @pl.when(at(i - 5))
         def _():
-            for a in (1, 0):
-                finish(scatter_rest(i - 5, a))
+            for a in (0, 1):
+                await_rest(i - 5, a)
                 sum_last(i - 5, a)
 
         @pl.when(at(i - 2))
         def _():
-            finish(share(i - 2, 0))
-            start(pass_on(i - 2))
+            for b in (0, 1):
+                finish(share(i - 2, b, 0))
+                start(pass_on(i - 2, b))
 
         return carry
 
     lax.fori_loop(0, CHUNKS + 4, step, 0)
 
-    finish(scatter_rest(CHUNKS - 1, 1))
-    sum_last(CHUNKS - 1, 1)
-    inv = invb[:, 0:1]
-    pull = jnp.sum(tokb[...].astype(F32) * gainb[0:1, :] * bw[...], axis=1, keepdims=True)
-    rmsb[y] = to_lanes(pull * inv)
-    sends = [rc(rmsb.at[y], rmsb.at[y], m_s.at[j - 1], m_r.at[j - 1], ydev(j)) for j in (1, 2, 3)]
-    start(sends)
-    finish(scatter_rest(CHUNKS - 1, 0))
+    await_rest(CHUNKS - 1, 0)
     sum_last(CHUNKS - 1, 0)
-    mixb[...] = (tokb[...].astype(F32) + fw[...]).astype(BF)
-    back = [
-        rc(mixb.at[:, theirs], mixed_ref.at[my_rows, :], o_s.at[0], o_r.at[0], twin),
-        rc(igb.at[:, theirs], ig_ref.at[my_rows, :], o_s.at[1], o_r.at[1], twin),
-    ]
-    start(back[0:1])
-    mixed_ref[my_rows, :] = mixb[:, mine]
-    finish(sends)
-    fix = inv * inv * to_column(((rmsb[0] + rmsb[1]) + (rmsb[2] + rmsb[3]))[0:1, :]) / MODEL
-    igb[...] = (
-        cotb[...].astype(F32) + gainb[0:1, :] * (inv * bw[...]) - tokb[...].astype(F32) * fix
-    ).astype(BF)
-    start(back[1:2])
-    ig_ref[my_rows, :] = igb[:, mine]
-
     finish(exchange)
 
     @pl.loop(0, 4)
@@ -457,7 +522,8 @@
             total = acc_d[rows, src] + recv_d[rows, cols].astype(F32)
             dg_ref[rows, cols] = (total * dm_ref[j, i].astype(F32)).astype(BF)
 
-    finish(back)
+    await_rest(CHUNKS - 1, 1)
+    sum_last(CHUNKS - 1, 1)
 
 
 def store(*refs):
@@ -471,6 +537,7 @@
 def shards(tokens, cotangent, norm_gain, gate_w, up_w, down_w, gate_b, up_b, down_b):
     vmem = pl.BlockSpec(memory_space=pltpu.VMEM)
     smem = pl.BlockSpec(memory_space=pltpu.SMEM)
+    hbm = pl.BlockSpec(memory_space=pltpu.HBM)
 
     def dma(*shape):
         return [pltpu.SemaphoreType.DMA(shape)] * 2
@@ -485,16 +552,23 @@
             V(up_w.shape, BF),
             V(down_w.shape, BF),
         ),
-        in_specs=[vmem] * 6 + [smem] * 3,
+        in_specs=[hbm, hbm, vmem, hbm, hbm, hbm] + [smem] * 3,
         out_specs=(vmem,) * 5,
         scratch_shapes=[
+            V((WIDE, FF), BF),
+            V((WIDE, FF), BF),
+            V((FF, WIDE), BF),
+            V((2 * HALF, WIDE), BF),
+            V((2 * HALF, WIDE), BF),
             V((HALF, CHIP), BF),
             V((HALF, CHIP), BF),
             V((8, WIDE), F32),
             V((8, CHIP), F32),
             V((4, 8, 128), F32),
             V((HALF, 128), F32),
-            V((4, 8, 128), F32),
+            V((2 * HALF, 128), F32),
+            V((CHUNKS, 4, 8, 128), F32),
+            V((2 * HALF, 128), F32),
             V((CHUNKS, 4, 4, TOK, 2 * CHIP), BF),
             V((CHIP, GU), BF),
             V((FF, CHIP), BF),
@@ -502,12 +576,10 @@
             V((CHUNKS, 2, 32, ALL), BF),
             V((CHUNKS, 2, 64, ALL), BF),
             V((CHUNKS, 4, 64, ALL), BF),
-            V((2, 4, 4, TOK, 2 * CHIP), BF),
-            V((CHUNKS, 2, 2, 3, 4, TOK, WIDE), BF),
-            V((CHUNKS, 2, 2, 4, TOK, WIDE), BF),
-            V((CHUNKS, 2, 2, 3, TOK, WIDE), BF),
-            V((HALF, CHIP), F32),
-            V((HALF, CHIP), F32),
+            V((2, 4, 4, TOK, 2 * (WIDE + 128) + CHIP), BF),
+            V((CHUNKS, 2, 2, 3, 4, TOK, WIDE + 128), BF),
+            V((CHUNKS, 2, 2, 4, TOK, WIDE + 128), BF),
+            V((CHUNKS, 2, 2, 4, TOK, WIDE + 128), BF),
             V((CHIP, GU), F32),
             V((FF, CHIP), F32),
             V((CHIP, 256), BF),
@@ -516,24 +588,22 @@
             V((FF, WIDE), BF),
             V((WIDE, GU), BF),
             V((FF, WIDE), BF),
-            V((HALF, CHIP), BF),
-            V((HALF, CHIP), BF),
+            pltpu.SemaphoreType.DMA((5,)),
         ]
-        + dma(5)
+        + dma(6)
         + dma(3)
         + dma(CHUNKS, 2, 2, 3)
         + dma(CHUNKS, 2, 2, 3)
         + dma(CHUNKS, 2, 2)
         + dma(CHUNKS, 2, 2)
+        + dma(CHUNKS, 3)
+        + dma(CHUNKS, 2, 2, 2)
         + dma(CHUNKS, 2, 2)
-        + dma(CHUNKS, 2)
         + dma(CHUNKS, 2, 2, 3)
-        + dma(CHUNKS, 2, 2, 3)
-        + dma(2)
-        + dma(3)
+        + dma(CHUNKS, 2, 2, 4)
         + dma(2),
         compiler_params=pltpu.CompilerParams(
-            collective_id=0, has_side_effects=True, vmem_limit_bytes=54 * 1024 * 1024
+            collective_id=0, has_side_effects=True, vmem_limit_bytes=56 * 1024 * 1024
         ),
         cost_estimate=pl.CostEstimate(flops=17_000_000_000, bytes_accessed=6_000_000, transcendentals=2_000_000),
         name="ffn",

time: 142 us -> 137 us (0.965)
  Pallas kernels: 142 us -> 136 us
    pallas_call x1, Pallas kernels: 140 us -> 134 us  [shards(): pl.pallas_call(body, out_shape=(V(tokens.shape, BF), V(tokens.shape, BF),...]
where the time goes in v3:
time: 137 us; the launch traced here: 136 us
  Pallas kernels  136 us (99%)
    pallas_call x1, Pallas kernels, shards(): pl.pallas_call(body, out_shape=(V(tokens.shape, BF), V(tokens.shape, BF),...  134 us

profile of v3, /device:TPU:1, one launch (start us, length us, event | category | flops | bytes accessed | tf_op | source)
XLA Modules:
  0.0 136.4 jit_solution(16914495699934583985)
XLA Ops:
  0.6 134.1 %ffn.1 = (bf16[128,512]{1,0:T(8,128)(2,1)S(1)}, bf16[128,512]{1,0:T(8,128)(2,1)S(1)}, bf16[512,896]{1,0:T(8,128)(2,1)S(1)}, bf16[512,896]{1,0:T(8,128)(2,1)S(1)}, bf16[896,512]{1,0:T(8,128)(2,1)S(1)}) custom-call(bf16[128,512]{1,0:T(8,128)(2,1)} %tok_ref.1, bf16[128,512]{1,0:T(8,128)(2,1)} %cot_ref.1, f32[1,512]{1,0:T(1,128)} %bitcast.2, ...), custom_call_target="tpu_custom_call" | custom-call | flops 16999999488 | bytes 6000000 | tf_op jit(solution)/shard_map/ffn/pallas_call | solution.py:546
  134.8 1.7 %store.1 = (bf16[128,512]{1,0:T(8,128)(2,1)}, bf16[128,512]{1,0:T(8,128)(2,1)}, bf16[512,896]{1,0:T(8,128)(2,1)}, bf16[512,896]{1,0:T(8,128)(2,1)}, bf16[896,512]{1,0:T(8,128)(2,1)}) custom-call(bf16[128,512]{1,0:T(8,128)(2,1)S(1)} %get-tuple-element.10.refs_0_, bf16[128,512]{1,0:T(8,128)(2,1)S(1)} %get-tuple-element.11.refs_1_, ...), custom_call_target="tpu_custom_call" | custom-call | tf_op jit(solution)/shard_map/store/pallas_call | solution.py:611

commit v4 on v3

--- a/solution.py
+++ b/solution.py
@@ -32,11 +32,10 @@
 def body(
     tok_ref, cot_ref, gain_ref, gw_ref, uw_ref, dw_ref, gm_ref, um_ref, dm_ref,
     mixed_ref, ig_ref, gg_ref, ug_ref, dg_ref,
-    gwb, uwb, dwb, tokn, cotn, tokb, cotb, gain8, gainb, ssq, invb, invn, pulls, totals,
+    gwb, uwb, dwb, tokn, cotn, xn, gain8, ssq, invn, pulls, totals,
     gath, wgu, wd, part, rel, full, hid, outp, rs1, sum1, rs2,
     acc_gu, acc_d, xt, ht, send_gu, send_d, recv_gu, recv_d,
-    l_s, sw_s, sw_r, sq_s, sq_r, p1_s, p1_r, p2_s, p2_r, r_s, r_r, f_s, f_r, t_s, t_r, g_s, g_r, h_s, h_r,
-    a_s, a_r, b_s, b_r, w_s, w_r,
+    l_s, w_s, w_r, p1_r, p2_r, r_s, r_r, f_s, f_r, t_r, g_r, h_r, a_s, a_r, b_r, q_r, gath_s, hid_s, sum_s, line_s,
 ):
     row = lax.axis_index("row")
     col = lax.axis_index("col")
@@ -72,26 +71,34 @@
         for copy in copies:
             copy.wait()
 
+    def tiles(count):
+        across = max(n for n in range(1, 15) if count % n == 0)
+        return acc_gu.at[pl.ds(0, 8 * (count // across)), pl.ds(0, 128 * across)]
+
+    def arrive(sem, count):
+        rc(tiles(count), tiles(count), sem, sem, twin).wait_recv()
+
+    def leave(sem, count):
+        rc(tiles(count), tiles(count), sem, sem, twin).wait_send()
+
     lo = pl.ds(0, CHIP)
     hi = pl.ds(CHIP, CHIP)
 
     def strip(a, h):
         return pl.ds(a * CHIP + h * WIDE, WIDE)
 
-    spot = lax.broadcasted_iota(jnp.int32, (HALF, 128), 0) == lax.broadcasted_iota(jnp.int32, (HALF, 128), 1)
-
     def to_lanes(column):
-        line = jnp.sum(jnp.where(spot, jnp.broadcast_to(column, (HALF, 128)), 0.0), axis=0, keepdims=True)
+        n = column.shape[0]
+        spot = lax.broadcasted_iota(jnp.int32, (n, 128), 0) == lax.broadcasted_iota(jnp.int32, (n, 128), 1)
+        line = jnp.sum(jnp.where(spot, jnp.broadcast_to(column, (n, 128)), 0.0), axis=0, keepdims=True)
         return jnp.broadcast_to(line, (8, 128))
 
-    def to_column(line):
-        return jnp.sum(jnp.where(spot, jnp.broadcast_to(line, (HALF, 128)), 0.0), axis=1, keepdims=True)
+    def to_column(line, n):
+        spot = lax.broadcasted_iota(jnp.int32, (n, 128), 0) == lax.broadcasted_iota(jnp.int32, (n, 128), 1)
+        return jnp.sum(jnp.where(spot, jnp.broadcast_to(line, (n, 128)), 0.0), axis=1, keepdims=True)
 
     mine = pl.ds(pl.multiple_of(c * WIDE, WIDE), WIDE)
     theirs = pl.ds(pl.multiple_of(other * WIDE, WIDE), WIDE)
-    my_rows = pl.ds(pl.multiple_of(c * HALF, HALF), HALF)
-    their_rows = pl.ds(pl.multiple_of(other * HALF, HALF), HALF)
-
     def width(a):
         return WIDE + 128 * (1 - a)
 
@@ -100,6 +107,7 @@
 
     barrier = pltpu.get_barrier_semaphore()
     peers = [twin] + [f(j) for f in (xdev, ydev, zdev) for j in (1, 2, 3)]
+    peers += [dev(z, x, (y + j) % 4, other) for j in (1, 2, 3)]
     peers += [dev((z + j) % 4, x, y, other) for j in (1, 2, 3)] + [dev(z, (x + j) % 4, y, other) for j in (1, 2, 3)]
     for peer in peers:
         pl.semaphore_signal(barrier, inc=1, device_id=peer, device_id_type=MESH)
@@ -112,11 +120,7 @@
     ]
     start(loads)
     gain8[...] = jnp.broadcast_to(gain_ref[...], (8, WIDE))
-    gainb[:, mine] = gain8[...]
-    finish(loads[0:2])
-    tokb[:, mine] = tokn[my_rows, :]
-    cotb[:, mine] = cotn[my_rows, :]
-    finish(loads[2:3])
+    finish(loads[0:3])
 
     @pl.loop(0, 7)
     def _(i):
@@ -128,40 +132,56 @@
 
     pl.semaphore_wait(barrier, len(peers))
 
-    swaps = [
-        rc(cotn.at[their_rows, :], cotb.at[:, mine], sw_s.at[0], sw_r.at[0], twin),
-        rc(tokn.at[their_rows, :], tokb.at[:, mine], sw_s.at[1], sw_r.at[1], twin),
-        rc(gain8, gainb.at[:, mine], sw_s.at[2], sw_r.at[2], twin),
-        rc(wd.at[:, mine], wd.at[:, mine], sw_s.at[3], sw_r.at[3], twin),
-        rc(wgu.at[mine, :], wgu.at[mine, :], sw_s.at[4], sw_r.at[4], twin),
-        rc(invn.at[my_rows, :], invn.at[my_rows, :], sw_s.at[5], sw_r.at[5], twin),
-    ]
-    start(swaps[0:4])
+    own = (xn, cotn)
+
+    def at_strip(a, core):
+        return pl.ds(pl.multiple_of(a * CHIP + core * WIDE, WIDE), WIDE)
 
     def near(k, a):
-        def one(h, to, j):
-            block = gath.at[k, z, x, :, strip(a, h)]
-            return rc(block, block, p1_s.at[k, a, h, j - 1], p1_r.at[k, a, h, j - 1], to(j))
-
-        return [one(h, to, j) for j in (1, 2, 3) for h, to in ((0, xdev), (1, zdev))]
+        def one(core, to):
+            rows = pl.ds(pl.multiple_of(core * HALF + k * TOK, TOK), TOK)
+            return rc(own[a].at[rows, :], gath.at[k, z, x, :, at_strip(a, c)], gath_s.at[k], p1_r.at[k, a], to)
+
+        far = [
+            one(core, dev((z + c * j) % 4, (x + other * j) % 4, y, core)) for j in (1, 2, 3) for core in (0, 1)
+        ]
+        return far + [one(other, twin)]
+
+    def keep(a):
+        for k in range(CHUNKS):
+            rows = pl.ds(pl.multiple_of(c * HALF + k * TOK, TOK), TOK)
+            gath[k, z, x, :, at_strip(a, c)] = own[a][rows, :]
 
     def rest(k, a):
         def one(h, to, j):
             block = gath.at[k, z, :, :, strip(a, 0)] if h == 0 else gath.at[k, :, x, :, strip(a, 1)]
-            return rc(block, block, p2_s.at[k, a, h, j - 1], p2_r.at[k, a, h, j - 1], to(j))
+            return rc(block, block, gath_s.at[k], p2_r.at[k, a], to(j))
 
         return [one(h, to, j) for j in (1, 2, 3) for h, to in ((0, zdev), (1, xdev))]
 
-    finish(swaps[0:1])
-    for k in range(CHUNKS):
-        gath[k, z, x, :, hi] = cotb[k * TOK : (k + 1) * TOK, :]
+    def near_here(k, a):
+        arrive(p1_r.at[k, a], 28)
+
+    def rest_here(k, a):
+        arrive(p2_r.at[k, a], 96)
+
     start(near(0, 1))
-
-    finish(swaps[1:3])
-    tok = tokb[...].astype(F32)
-    ssq[y] = to_lanes(jnp.sum(tok * tok, axis=1, keepdims=True))
-    sends = [rc(ssq.at[y], ssq.at[y], sq_s.at[j - 1], sq_r.at[j - 1], ydev(j)) for j in (1, 2, 3)]
-    start(sends)
+    tok = tokn[...].astype(F32)
+    ssq[col] = to_lanes(jnp.sum(tok * tok, axis=1, keepdims=True))
+    start(
+        [
+            rc(ssq.at[col], ssq.at[col], line_s.at[0], q_r.at[0], to)
+            for to in [twin] + [dev(z, x, (y + j) % 4, core) for j in (1, 2, 3) for core in (0, 1)]
+        ]
+    )
+    exchange = [
+        rc(wd.at[:, mine], wd.at[:, mine], w_s.at[0], w_r.at[0], twin),
+        rc(wgu.at[mine, :], wgu.at[mine, :], w_s.at[1], w_r.at[1], twin),
+        rc(send_gu, recv_gu, w_s.at[2], w_r.at[2], twin),
+        rc(send_d, recv_d, w_s.at[3], w_r.at[3], twin),
+    ]
+    start(exchange[0:1])
+    keep(1)
     finish(loads[3:5])
 
     @pl.loop(0, 4)
@@ -175,29 +195,28 @@
             keep = um_ref[i, j].astype(F32)
             wgu[to, FF + j * 128 : FF + j * 128 + 128] = (uwb[rows, cols].astype(F32) * keep).astype(BF)
 
-    start(swaps[4:5])
-    finish(near(0, 1))
+    start(exchange[1:2])
+    near_here(0, 1)
     start(rest(0, 1))
-    finish(sends)
-    squares = to_column(((ssq[0] + ssq[1]) + (ssq[2] + ssq[3]))[0:1, :])
-    invb[...] = jnp.broadcast_to(1.0 / jnp.sqrt(squares / MODEL + epsilon), (HALF, 128))
-    for k in range(CHUNKS):
-        rows = slice(k * TOK, (k + 1) * TOK)
-        scaled = tokb[rows, :].astype(F32) * gainb[0:1, :] * invb[rows, 0:1]
-        gath[k, z, x, :, lo] = scaled.astype(BF)
+    arrive(q_r.at[0], 7)
+    squares = ssq[0]
+    for n in range(1, 8):
+        squares += ssq[n]
+    inv = 1.0 / jnp.sqrt(to_column(squares[0:1, :], 128) / MODEL + epsilon)
+    invn[...] = jnp.broadcast_to(inv, (2 * HALF, 128))
+    xn[...] = (tokn[...].astype(F32) * gain8[0:1, :] * inv).astype(BF)
     start(near(0, 0))
-    invn[my_rows, :] = invb[...]
-    start(swaps[5:6])
+    keep(0)
 
     @pl.loop(0, 16)
     def _(i):
         acc_gu[pl.ds(pl.multiple_of(i * 64, 64), 64), :] = jnp.zeros((64, GU), F32)
         acc_d[pl.ds(pl.multiple_of(i * 56, 56), 56), :] = jnp.zeros((56, CHIP), F32)
 
-    finish(near(0, 0))
+    near_here(0, 0)
     start(rest(0, 0))
     start(near(1, 1) + near(1, 0))
-    finish(swaps[3:6])
+    finish(exchange[0:2])
 
     def span(a):
         return pl.ds(GU, FF) if a == 1 else pl.ds(0, GU)
@@ -206,14 +225,14 @@
         one = part.at[s, op, pl.ds(0, 32), span(a)]
         two = part.at[s, op, pl.ds(32, 32), span(a)]
         return [
-            rc(one, rel.at[k, 0, :, span(a)], r_s.at[k, a, 0], r_r.at[k, a, 0], up_dev),
-            rc(two, rel.at[k, 1, :, span(a)], r_s.at[k, a, 1], r_r.at[k, a, 1], dn_dev),
+            rc(one, rel.at[k, 0, :, span(a)], r_s.at[k, a], r_r.at[k, a], up_dev),
+            rc(two, rel.at[k, 1, :, span(a)], r_s.at[k, a], r_r.at[k, a], dn_dev),
         ]
 
     def quarter(k, s, a):
         return [
-            rc(part.at[s, up, :, span(a)], full.at[k, 0, :, span(a)], f_s.at[k, a, 0], f_r.at[k, a, 0], up_dev),
-            rc(part.at[s, dn, :, span(a)], full.at[k, 1, :, span(a)], f_s.at[k, a, 1], f_r.at[k, a, 1], dn_dev),
+            rc(part.at[s, up, :, span(a)], full.at[k, 0, :, span(a)], f_s.at[k], f_r.at[k], up_dev),
+            rc(part.at[s, dn, :, span(a)], full.at[k, 1, :, span(a)], f_s.at[k], f_r.at[k], dn_dev),
         ]
 
     def kind(b):
@@ -223,20 +242,20 @@
         one = hid.at[k, y, pl.ds(32 if later else 0, 32), kind(b)]
         two = hid.at[k, y, pl.ds(0 if later else 32, 32), kind(b)]
         return [
-            rc(one, one, g_s.at[k, b, later, 0], g_r.at[k, b, later, 0], up_dev),
-            rc(two, two, g_s.at[k, b, later, 1], g_r.at[k, b, later, 1], dn_dev),
+            rc(one, one, hid_s.at[k], g_r.at[k, b, later], up_dev),
+            rc(two, two, hid_s.at[k], g_r.at[k, b, later], dn_dev),
         ]
 
     def pass_on(k, b):
         first = hid.at[k, dn, pl.ds(0, 32), kind(b)]
         second = hid.at[k, up, pl.ds(32, 32), kind(b)]
         return [
-            rc(first, first, h_s.at[k, b, 0], h_r.at[k, b, 0], up_dev),
-            rc(second, second, h_s.at[k, b, 1], h_r.at[k, b, 1], dn_dev),
+            rc(first, first, hid_s.at[k], h_r.at[k, b], up_dev),
+            rc(second, second, hid_s.at[k], h_r.at[k, b], dn_dev),
         ]
 
     def tell(k):
-        return [rc(pulls.at[k, y], pulls.at[k, y], t_s.at[k, j - 1], t_r.at[k, j - 1], ydev(j)) for j in (1, 2, 3)]
+        return [rc(pulls.at[k, y], pulls.at[k, y], line_s.at[0], t_r.at[k], ydev(j)) for j in (1, 2, 3)]
 
     def scatter(k, s, a):
         def one(h, to, j):
@@ -244,7 +263,7 @@
             block = outp.at[s, :, (x + j) % 4, :, strip_a] if h == 0 else outp.at[s, (z + j) % 4, :, :, strip_a]
             return rc(
                 block, rs1.at[k, a, h, j - 1, :, :, pl.ds(0, width(a))],
-                a_s.at[k, a, h, j - 1], a_r.at[k, a, h, j - 1], to(j),
+                a_s.at[k, a], a_r.at[k, a], to(j),
             )
 
         return [one(h, to, j) for j in (1, 2, 3) for h, to in ((0, xdev), (1, zdev))]
@@ -253,31 +272,21 @@
     at_theirs = z * c + x * other
 
     def scatter_rest(k, a):
-        def one(h, place, send, j, to):
+        def one(h, place, j, to):
             return rc(
                 sum1.at[k, a, h, place, :, pl.ds(0, width(a))], rs2.at[k, a, c, j, :, pl.ds(0, width(a))],
-                send, b_r.at[k, a, c, j], to,
+                sum_s.at[0], b_r.at[k, a], to,
             )
 
         far = [
-            one(h, ((x if h else z) + j) % 4, b_s.at[k, a, h, j], j,
+            one(h, ((x if h else z) + j) % 4, j,
                 dev(z, (x + j) % 4, y, 1) if h else dev((z + j) % 4, x, y, 0))
             for j in (1, 2, 3) for h in (0, 1)
         ]
-        return far + [one(other, at_theirs, b_s.at[k, a, 0, 0], 0, twin)]
+        return far + [one(other, at_theirs, 0, twin)]
 
     def await_rest(k, a):
-        for copy in scatter_rest(k, a):
-            copy.wait_send()
-
-        def arrival(core, j):
-            place = rs2.at[k, a, core, j, :, pl.ds(0, width(a))]
-            rc(place, place, b_s.at[k, a, 0, 0], b_r.at[k, a, core, j], twin).wait_recv()
-
-        arrival(other, 0)
-        for j in (1, 2, 3):
-            arrival(0, j)
-            arrival(1, j)
+        arrive(b_r.at[k, a], 28 if a == 1 else 35)
 
     def project_pre(k):
         s = k % 2
@@ -345,7 +354,7 @@
             outp[s, :, :, :, to] = got.astype(BF).reshape(4, 4, TOK, 256)
 
         for i in range(4):
-            pulled = jnp.broadcast_to(to_column(pulls[k, i, 0:1, :]), (HALF, 128)).astype(BF).reshape(4, TOK, 128)
+            pulled = jnp.broadcast_to(to_column(pulls[k, i, 0:1, :], HALF), (HALF, 128)).astype(BF).reshape(4, TOK, 128)
             outp[s, i, :, :, WIDE : WIDE + 128] = pulled
             outp[s, i, :, :, 2 * WIDE + 128 : 2 * WIDE + 256] = pulled
 
@@ -396,11 +405,6 @@
                     cotn[rows, :].astype(F32) + gain8[0:1, :] * (inv * total) - tokn[rows, :].astype(F32) * fix
                 ).astype(BF)
 
-    exchange = [
-        rc(send_gu, recv_gu, w_s.at[0], w_r.at[0], twin),
-        rc(send_d, recv_d, w_s.at[1], w_r.at[1], twin),
-    ]
-
     def step(i, carry):
         def at(k):
             return jnp.logical_and(k >= 0, k < CHUNKS)
@@ -408,8 +412,8 @@
         @pl.when(at(i - 2))
         def _():
             k = i - 2
-            finish(quarter(k, k % 2, 1))
-            finish(quarter(k, k % 2, 0))
+            leave(f_s.at[k], 168)
+            arrive(f_r.at[k], 168)
             activate(k)
             start(tell(k))
             for b in (0, 1):
@@ -419,23 +423,24 @@
         def _():
             k = i - 1
             for a in (1, 0):
-                finish(relay(k, k % 2, a))
+                leave(r_s.at[k, a], 28 if a == 1 else 56)
+                arrive(r_r.at[k, a], 28 if a == 1 else 56)
                 add_relay(k, a)
                 start(quarter(k, k % 2, a))
 
         @pl.when(i < CHUNKS)
         def _():
-            finish(rest(i, 1))
+            rest_here(i, 1)
             project_back(i)
             start(relay(i, i % 2, 1))
-            finish(rest(i, 0))
+            rest_here(i, 0)
             project_pre(i)
             start(relay(i, i % 2, 0))
 
         @pl.when(i + 1 < CHUNKS)
         def _():
             for a in (1, 0):
-                finish(near(i + 1, a))
+                near_here(i + 1, a)
                 start(rest(i + 1, a))
 
         @pl.when(i + 2 < CHUNKS)
@@ -446,14 +451,17 @@
         def _():
             k = i - 4
             for a in (0, 1):
-                finish(scatter(k, k % 2, a))
+                leave(a_s.at[k, a], 96 if a == 1 else 120)
+                arrive(a_r.at[k, a], 96 if a == 1 else 120)
                 sum_first(k, a)
                 start(scatter_rest(k, a))
 
         @pl.when(at(i - 3))
         def _():
             k = i - 3
-            finish(tell(k) + share(k, 0, 1) + pass_on(k, 0))
+            arrive(t_r.at[k], 3)
+            arrive(g_r.at[k, 0, 1], 28)
+            arrive(h_r.at[k, 0], 28)
             products_out(k)
             start(scatter(k, k % 2, 0))
             sums_d(k)
@@ -461,12 +469,13 @@
         @pl.when(i - 3 == CHUNKS - 1)
         def _():
             send_d[...] = acc_d[:, theirs].astype(BF)
-            start(exchange[1:])
+            start(exchange[3:4])
 
         @pl.when(at(i - 3))
         def _():
             k = i - 3
-            finish(share(k, 1, 1) + pass_on(k, 1))
+            arrive(g_r.at[k, 1, 1], 56)
+            arrive(h_r.at[k, 1], 56)
             products_back(k)
             start(scatter(k, k % 2, 1))
             sums_gu(k)
@@ -479,7 +488,7 @@
                 src = pl.ds(pl.multiple_of(other * WIDE + n * 128, 128), 128)
                 send_gu[rows, :] = acc_gu[src, :].astype(BF)
 
-            start(exchange[0:1])
+            start(exchange[2:3])
 
         @pl.when(at(i - 5))
         def _():
@@ -490,7 +499,7 @@
         @pl.when(at(i - 2))
         def _():
             for b in (0, 1):
-                finish(share(i - 2, b, 0))
+                arrive(g_r.at[i - 2, b, 0], 28 * (1 + b))
                 start(pass_on(i - 2, b))
 
         return carry
@@ -499,7 +508,7 @@
 
     await_rest(CHUNKS - 1, 0)
     sum_last(CHUNKS - 1, 0)
-    finish(exchange)
+    finish(exchange[2:4])
 
     @pl.loop(0, 4)
     def _(i):
@@ -524,6 +533,11 @@
 
     await_rest(CHUNKS - 1, 1)
     sum_last(CHUNKS - 1, 1)
+    for k in range(CHUNKS):
+        leave(gath_s.at[k], 2 * (28 + 96))
+        leave(hid_s.at[k], 3 * (28 + 56))
+    leave(sum_s.at[0], CHUNKS * (28 + 35))
+    leave(line_s.at[0], 7 + CHUNKS * 3)
 
 
 def store(*refs):
@@ -540,7 +554,7 @@
     hbm = pl.BlockSpec(memory_space=pltpu.HBM)
 
     def dma(*shape):
-        return [pltpu.SemaphoreType.DMA(shape)] * 2
+        return pltpu.SemaphoreType.DMA(shape)
 
     V = pltpu.VMEM
     results = pl.pallas_call(
@@ -560,12 +574,9 @@
             V((FF, WIDE), BF),
             V((2 * HALF, WIDE), BF),
             V((2 * HALF, WIDE), BF),
-            V((HALF, CHIP), BF),
-            V((HALF, CHIP), BF),
+            V((2 * HALF, WIDE), BF),
             V((8, WIDE), F32),
-            V((8, CHIP), F32),
-            V((4, 8, 128), F32),
-            V((HALF, 128), F32),
+            V((8, 8, 128), F32),
             V((2 * HALF, 128), F32),
             V((CHUNKS, 4, 8, 128), F32),
             V((2 * HALF, 128), F32),
@@ -588,20 +599,27 @@
             V((FF, WIDE), BF),
             V((WIDE, GU), BF),
             V((FF, WIDE), BF),
-            pltpu.SemaphoreType.DMA((5,)),
-        ]
-        + dma(6)
-        + dma(3)
-        + dma(CHUNKS, 2, 2, 3)
-        + dma(CHUNKS, 2, 2, 3)
-        + dma(CHUNKS, 2, 2)
-        + dma(CHUNKS, 2, 2)
-        + dma(CHUNKS, 3)
-        + dma(CHUNKS, 2, 2, 2)
-        + dma(CHUNKS, 2, 2)
-        + dma(CHUNKS, 2, 2, 3)
-        + dma(CHUNKS, 2, 2, 4)
-        + dma(2),
+            dma(5),
+            dma(4),
+            dma(4),
+            dma(CHUNKS, 2),
+            dma(CHUNKS, 2),
+            dma(CHUNKS, 2),
+            dma(CHUNKS, 2),
+            dma(CHUNKS),
+            dma(CHUNKS),
+            dma(CHUNKS),
+            dma(CHUNKS, 2, 2),
+            dma(CHUNKS, 2),
+            dma(CHUNKS, 2),
+            dma(CHUNKS, 2),
+            dma(CHUNKS, 2),
+            dma(1),
+            dma(CHUNKS),
+            dma(CHUNKS),
+            dma(1),
+            dma(1),
+        ],
         compiler_params=pltpu.CompilerParams(
             collective_id=0, has_side_effects=True, vmem_limit_bytes=56 * 1024 * 1024
         ),

time: 137 us -> 133 us (0.971)
  Pallas kernels: 136 us -> 132 us
    pallas_call x1, Pallas kernels: 134 us -> 130 us  [shards(): pl.pallas_call(body, out_shape=(V(tokens.shape, BF), V(tokens.shape, BF),...]
where the time goes in v4:
time: 133 us; the launch traced here: 132 us
  Pallas kernels  132 us (99%)
    pallas_call x1, Pallas kernels, shards(): pl.pallas_call(body, out_shape=(V(tokens.shape, BF), V(tokens.shape, BF),...  130 us

profile of v4, /device:TPU:1, one launch (start us, length us, event | category | flops | bytes accessed | tf_op | source)
XLA Modules:
  0.0 132.5 jit_solution(4829228885500236559)
XLA Ops:
  0.6 130.2 %ffn.1 = (bf16[128,512]{1,0:T(8,128)(2,1)S(1)}, bf16[128,512]{1,0:T(8,128)(2,1)S(1)}, bf16[512,896]{1,0:T(8,128)(2,1)S(1)}, bf16[512,896]{1,0:T(8,128)(2,1)S(1)}, bf16[896,512]{1,0:T(8,128)(2,1)S(1)}) custom-call(bf16[128,512]{1,0:T(8,128)(2,1)} %tok_ref.1, bf16[128,512]{1,0:T(8,128)(2,1)} %cot_ref.1, f32[1,512]{1,0:T(1,128)} %bitcast.2, ...), custom_call_target="tpu_custom_call" | custom-call | flops 16999999488 | bytes 6000000 | tf_op jit(solution)/shard_map/ffn/pallas_call | solution.py:560
  130.8 1.7 %store.1 = (bf16[128,512]{1,0:T(8,128)(2,1)}, bf16[128,512]{1,0:T(8,128)(2,1)}, bf16[512,896]{1,0:T(8,128)(2,1)}, bf16[512,896]{1,0:T(8,128)(2,1)}, bf16[896,512]{1,0:T(8,128)(2,1)}) custom-call(bf16[128,512]{1,0:T(8,128)(2,1)S(1)} %get-tuple-element.10.refs_0_, bf16[128,512]{1,0:T(8,128)(2,1)S(1)} %get-tuple-element.11.refs_1_, ...), custom_call_target="tpu_custom_call" | custom-call | tf_op jit(solution)/shard_map/store/pallas_call | solution.py:629
